TPU v7x, 256 devices: a whole 4x4x8 slice. The times are simulated.
256 devices in a mesh: row: 4 (over y), col: 16 (over x, z_lo, core), depth: 4 (over z_hi).
Axes of the slice: x: 4, y: 4, z: 8 (z_hi: 4, z_lo: 2; z = z_hi * 2 + z_lo), core: 2. Of those that a mesh axis runs over, the one named last changes fastest.
Arguments:
- coverage: bfloat16 [12288, 16384], P('row', 'col'), may hold values from 0 to 8
- block_mask: int32 [96, 128], P('row', 'col'), may hold values from 0 to 1
- edge_prior: bfloat16 [16384, 512], P('col', 'depth'), may hold values from 0.25 to 4
- test_cost: int32 [12288, 512], P('row', 'depth'), may hold values from 1 to 16
Outputs:
- edge_weights: float32 [16384, 512], P('col', 'depth')
- primal: float32 [12288, 512], P(('row', 'col'), 'depth')
All inputs are finite; a program needn't handle non-finite values.
Results may differ from a plain program's by a relative error of at most 0.0003.
Values may be sent and summed in bfloat16 or wider, within the bound.
No kernel may reach another device: no remote copies, remote signals or barrier semaphores. Data moves between devices by JAX's collectives and lax.ppermute only.
A program may use at most 64 MiB of HBM per device.

v0:
```python
import functools

import jax
import jax.numpy as jnp
from jax import lax
from jax.experimental import pallas as pl
from jax.experimental.pallas import tpu as pltpu
from jax.sharding import PartitionSpec as P

EDGES = 16384
SCEN = 512
BLOCK = 128
ITERS = 2
TESTS = 12288
CHUNK = 192
PAIR = 2 * CHUNK
HALF = 4 * PAIR
WITH_SUMS = PAIR + 8
GATHERED = PAIR + 32
VMEM_LIMIT = 16 * 1024 * 1024
IN_VMEM = pl.BlockSpec(memory_space=pltpu.VMEM)
IN_SMEM = pl.BlockSpec(memory_space=pltpu.SMEM)
ANYWHERE = pl.BlockSpec(memory_space=pl.ANY)
IN_HBM = pl.BlockSpec(memory_space=pltpu.HBM)
f32 = jnp.float32
bf16 = jnp.bfloat16


def call(kernel, out_shape, in_specs, out_specs, flops, scratch=()):
    return pl.pallas_call(
        kernel,
        in_specs=in_specs,
        out_specs=out_specs,
        out_shape=out_shape,
        scratch_shapes=list(scratch),
        compiler_params=pltpu.CompilerParams(vmem_limit_bytes=VMEM_LIMIT),
        cost_estimate=pl.CostEstimate(flops=flops, bytes_accessed=flops // 400, transcendentals=0),
    )


def in_vmem(value):
    return pltpu.with_memory_space_constraint(value, pltpu.VMEM)


def in_hbm(value):
    return pltpu.with_memory_space_constraint(value, pltpu.HBM)


def tests_of(kept_ref, d, half, edges=slice(None)):
    tests = kept_ref[half * 4 + d, :, :, edges]
    return tests.reshape(PAIR, tests.shape[-1])


def scores_and_sums(kept, weights, out_ref, d):
    at = d * WITH_SUMS
    out_ref[at : at + PAIR, :] = jnp.dot(kept, weights, preferred_element_type=f32)
    ones = jnp.ones((8, kept.shape[1]), bf16)
    sums = lax.dot_general(ones, kept, (((1,), (1,)), ((), ())), preferred_element_type=f32)
    out_ref[at + PAIR : at + WITH_SUMS, :] = jnp.concatenate(
        [sums[:1, j * BLOCK : (j + 1) * BLOCK] for j in range(3)] + [jnp.zeros((5, BLOCK), f32)], axis=0
    )


def first_scores_kernel(place_ref, mask_ref, cover_ref, prior_ref, out_ref, kept_ref, weights_ref, rows_ref, tiles_ref, sems):
    tiles = pltpu.make_async_copy(mask_ref, tiles_ref, sems.at[8])
    tiles.start()
    copies = {}
    for half in (1, 0):
        core = 1 - place_ref[1] if half else place_ref[1]
        for d in range(4):
            x = lax.rem(place_ref[0] + d, 4)
            copy = pltpu.make_async_copy(
                cover_ref.at[pl.ds(2 * x, 2), core], kept_ref.at[half * 4 + d], sems.at[half * 4 + d]
            )
            copy.start()
            copies[half, d] = copy
        if half:
            weights = pltpu.make_async_copy(prior_ref, weights_ref, sems.at[9])
            weights.start()
    edges = cover_ref.shape[-1]
    tiles.wait()
    column = lax.broadcasted_iota(jnp.int32, (tiles_ref.shape[0], edges), 1) // BLOCK
    spread = column == lax.broadcasted_iota(jnp.int32, column.shape, 0)
    rows_ref[...] = lax.dot_general(
        tiles_ref[...].astype(f32), spread.astype(f32), (((0,), (0,)), ((), ())), preferred_element_type=f32
    )
    weights.wait()
    lines = BLOCK // 2
    for half in (1, 0):
        core = 1 - place_ref[1] if half else place_ref[1]
        for d in range(4):
            copies[half, d].wait()
            for z in range(2):
                chunk = lax.rem(place_ref[0] + d, 4) * 4 + z * 2 + core
                for j in range(CHUNK // lines):
                    block_row = (chunk * (CHUNK // lines) + j) // 2
                    entry = jnp.broadcast_to(rows_ref[pl.ds(block_row, 1), :], (16, edges)).astype(bf16)
                    for k in range(lines // 16):
                        at = slice(j * lines + k * 16, j * lines + k * 16 + 16)
                        kept_ref[half * 4 + d, z, at, :] = kept_ref[half * 4 + d, z, at, :] * entry
            if half:
                scores_and_sums(tests_of(kept_ref, d, half), weights_ref[...], out_ref, d)


def own_scores_kernel(kept_ref, weights_ref, out_ref):
    for d in range(4):
        scores_and_sums(tests_of(kept_ref, d, 0), weights_ref[...], out_ref, d)


def first_scores(cover, mask, prior, place):
    edges, scen = prior.shape
    away, kept, weights = call(
        first_scores_kernel,
        [
            pltpu.VMEM((4 * WITH_SUMS, scen), f32),
            pltpu.VMEM((8, 2, CHUNK, edges), bf16),
            pltpu.VMEM(prior.shape, bf16),
        ],
        [IN_SMEM, IN_HBM, IN_HBM, IN_HBM],
        [IN_VMEM] * 3,
        2 * HALF * edges * scen,
        [
            pltpu.VMEM((mask.shape[0], edges), f32),
            pltpu.VMEM(mask.shape[::-1], mask.dtype),
            pltpu.SemaphoreType.DMA((10,)),
        ],
    )(place, in_hbm(mask.T), in_hbm(cover.reshape(-1, 2, CHUNK, edges)), in_hbm(prior))
    here = call(
        own_scores_kernel,
        pltpu.VMEM((4 * WITH_SUMS, scen), f32),
        [IN_VMEM, IN_VMEM],
        IN_VMEM,
        2 * HALF * edges * scen,
    )(in_vmem(kept), in_vmem(weights))
    return away, here, kept, weights


def scores_kernel(half, kept_ref, weights_ref, out_ref):
    for d in range(4):
        out_ref[d * PAIR : (d + 1) * PAIR, :] = jnp.dot(
            tests_of(kept_ref, d, half), weights_ref[...], preferred_element_type=f32
        )


def later_scores(half, kept, weights):
    edges, scen = weights.shape
    return call(
        functools.partial(scores_kernel, half),
        pltpu.VMEM((HALF, scen), f32),
        [IN_VMEM, IN_VMEM],
        IN_VMEM,
        2 * HALF * edges * scen,
    )(in_vmem(kept), in_vmem(weights))


def flip_kernel(place_ref, kept_ref, cost_ref, after_ref, own_out, other_out, cost_out, cost_in, sems):
    copies = []
    for z in range(2):
        at = pl.multiple_of((place_ref[0] * 4 + z * 2 + place_ref[1]) * CHUNK, CHUNK)
        copy = pltpu.make_async_copy(
            cost_ref.at[pl.ds(at, CHUNK), :], cost_in.at[pl.ds(z * CHUNK, CHUNK), :], sems.at[z]
        )
        copy.start()
        copies.append(copy)
    for half, out_ref in enumerate((own_out, other_out)):
        for d in range(4):
            out_ref[:, d * PAIR : (d + 1) * PAIR] = tests_of(kept_ref, (4 - d) % 4, half).T
    for copy in copies:
        copy.wait()
    cost_out[...] = cost_in[...].astype(f32)


def flip(kept, cost, place, after):
    edges = kept.shape[-1]
    return call(
        flip_kernel,
        [
            pltpu.VMEM((edges, HALF), bf16),
            pltpu.VMEM((edges, HALF), bf16),
            pltpu.VMEM((PAIR, cost.shape[1]), f32),
        ],
        [IN_SMEM, IN_VMEM, IN_HBM, ANYWHERE],
        [IN_VMEM, IN_VMEM, IN_VMEM],
        16 * HALF * edges * 128,
        [pltpu.VMEM((PAIR, cost.shape[1]), cost.dtype), pltpu.SemaphoreType.DMA((2,))],
    )(place, in_vmem(kept), in_hbm(cost), after)


def column_sums(low):
    return jnp.dot(jnp.ones((8, low.shape[0]), bf16), low, preferred_element_type=f32)


def add_loads(flipped_ref, low_ref, load, size):
    stride = low_ref.shape[0] // 4
    for d in range(4):
        low = low_ref[d * stride : d * stride + PAIR, :]
        load += jnp.dot(flipped_ref[:, d * PAIR : (d + 1) * PAIR], low, preferred_element_type=f32)
        size += column_sums(low)
    return load, size


def half_loads_kernel(flipped_ref, low_ref, load_ref, size_ref):
    load, size = add_loads(flipped_ref, low_ref, jnp.zeros(load_ref.shape, f32), jnp.zeros(size_ref.shape, f32))
    load_ref[...] = load
    size_ref[...] = size


def whole_loads_kernel(flipped_ref, low_ref, load_in, size_in, wire_ref):
    load, size = add_loads(flipped_ref, low_ref, load_in[...], size_in[...])
    power = jnp.floor(jnp.log2(jnp.maximum(size, 1e-30)))
    edges = load.shape[0]
    wire_ref[:edges, :] = load * jnp.exp2(11.0 - power[:1, :])
    wire_ref[edges:, :] = jnp.concatenate([power, power], axis=0)


def half_loads(flipped, low):
    edges, scen = flipped.shape[0], low.shape[1]
    return call(
        half_loads_kernel,
        [jax.ShapeDtypeStruct((edges, scen), f32), jax.ShapeDtypeStruct((8, scen), f32)],
        [IN_VMEM] * 2,
        [IN_VMEM, IN_VMEM],
        2 * HALF * edges * scen,
    )(in_vmem(flipped), low)


def whole_loads(flipped, low, load, size):
    edges, scen = load.shape
    return call(
        whole_loads_kernel,
        jax.ShapeDtypeStruct((edges + 16, scen), f32),
        [IN_VMEM] * 4,
        IN_VMEM,
        2 * HALF * edges * scen,
    )(in_vmem(flipped), low, load, size)


def total_kernel(sums_own, sums_away, low_own, low_away, out_ref):
    totals = [jnp.zeros((32, BLOCK), f32) for _ in range(3)]
    stride = low_own.shape[0] // 4
    for sums_ref, low_ref in ((sums_own, low_own), (sums_away, low_away)):
        for d in range(4):
            sums = sums_ref[d * GATHERED + PAIR : (d + 1) * GATHERED, :]
            for j in range(3):
                low = low_ref[d * stride + j * BLOCK : d * stride + (j + 1) * BLOCK, :]
                totals[j] += jnp.dot(sums, low, preferred_element_type=f32)
    row = lax.broadcasted_iota(jnp.int32, (32, BLOCK), 0)
    total = jnp.zeros((32, BLOCK), f32)
    for j in range(3):
        total += jnp.where(row % 8 == j, totals[j], 0.0)
    out_ref[...] = jnp.full(out_ref.shape, jnp.sum(total), f32)


def total_load(sums_own, sums_away, low_own, low_away):
    return call(
        total_kernel,
        jax.ShapeDtypeStruct((8, low_own.shape[1]), f32),
        [IN_VMEM] * 4,
        IN_VMEM,
        10**8,
    )(sums_own, sums_away, low_own, low_away)


def bf16_parts(sums):
    parts = []
    left = sums
    for _ in range(3):
        part = lax.reduce_precision(left, 8, 7)
        left = left - part
        parts.append(part)
    return parts + [jnp.zeros_like(sums)]


def pack_sums(value):
    return jnp.concatenate([value[:PAIR]] + bf16_parts(value[PAIR:]), axis=0).astype(bf16)


def unpack_sums(value):
    value = value.astype(f32)
    sums = value[PAIR : PAIR + 8] + value[PAIR + 8 : PAIR + 16] + value[PAIR + 16 : PAIR + 24]
    return jnp.concatenate([value[:PAIR], sums], axis=0)


def pack_int16(value):
    top = jnp.max(value, axis=0, keepdims=True)
    power = jnp.ceil(jnp.log2(jnp.maximum(top, 1e-30)))
    code = jnp.round(value * jnp.exp2(16.0 - power)) - 32768.0
    code = jnp.clip(code, -32768.0, 32767.0)
    tile = jnp.broadcast_to(power, (16, value.shape[1]))
    return jnp.concatenate([code, tile], axis=0).astype(jnp.int32).astype(jnp.int16)


def unpack_int16(value):
    value = value.astype(jnp.int32).astype(f32)
    return (value[:-16] + 32768.0) * jnp.exp2(value[-16:-15] - 16.0)


def to_float16(value):
    return lax.reduce_precision(value, 5, 10)


def update_kernel(last, place_ref, zero, one, two, three, total_ref, current_ref, *rest):
    edges = current_ref.shape[0]
    mean = total_ref[:1, :] * (1.0 / (EDGES * SCEN)) + 1e-06
    if last:
        ratios_ref, out_ref, primal_ref = rest
        own = ratios_ref[pl.ds(pl.multiple_of(place_ref[3] * CHUNK, CHUNK), CHUNK), :]
        primal_ref[...] = TESTS * own / mean
    else:
        out_ref, low_ref = rest
    wires = (zero, one, two, three)
    factors = [-0.25 * jnp.exp2(wire[edges : edges + 1, :] - 11.0) / mean for wire in wires]
    part = 128
    for n in range(edges // part):
        rows = slice(n * part, (n + 1) * part)
        loads = [wire[rows, :] * factor for wire, factor in zip(wires, factors, strict=True)]
        new = current_ref[rows, :].astype(f32) * jnp.exp((loads[0] + loads[2]) + (loads[1] + loads[3]))
        out_ref[rows, :] = new
        if not last:
            low_ref[rows, :] = new.astype(bf16)


def update(wires, total, current, place, ratios=None):
    edges, scen = current.shape
    last = ratios is not None
    if last:
        shapes = [jax.ShapeDtypeStruct((edges, scen), f32), jax.ShapeDtypeStruct((CHUNK, scen), f32)]
    else:
        shapes = [pltpu.VMEM((edges, scen), f32), pltpu.VMEM((edges, scen), bf16)]
    return call(
        functools.partial(update_kernel, last),
        shapes,
        [IN_SMEM] + [IN_VMEM] * (7 if last else 6),
        [IN_VMEM] * 2,
        10**7,
    )(place, *wires, total, in_vmem(current), *([ratios] if last else []))


def ring(n, d, stride=1):
    return [(i, (i + d * stride) % n) for i in range(n)]


def swap(bit):
    return [(i, i ^ bit) for i in range(16)]


def pair_sum(value, axis, bit):
    return value + lax.ppermute(value, axis, [(i, i ^ bit) for i in range(4)])


def sum_four(parts):
    zero, one, two, three = parts
    return (zero + two) + (one + three)


def body(coverage, block_mask, edge_prior, test_cost):
    at = lax.axis_index("col")
    x, z, core = at // 4, (at // 2) % 2, at % 2
    place = jnp.stack([x, core, lax.axis_index("row"), z]).astype(jnp.int32)
    for iteration in range(ITERS):
        first = iteration == 0
        pack, unpack = (pack_sums, unpack_sums) if first else (pack_int16, unpack_int16)
        with jax.named_scope("scores"):
            if first:
                away, here, kept, low_weights = first_scores(coverage, block_mask, edge_prior, place)
                current = low_weights
            else:
                away = later_scores(1, kept, low_weights)
                here = later_scores(0, kept, low_weights)
            here = here + lax.ppermute(away, "col", swap(1))
            here = here.reshape(4, -1, here.shape[-1])
        with jax.named_scope("sum_x"):
            parts = [unpack(lax.ppermute(pack(here[d]), "col", ring(16, d, 4))) for d in (1, 2, 3)]
            scores = sum_four([here[0]] + parts)
        if first:
            with jax.named_scope("flip"):
                flipped_here, flipped_away, cost = flip(kept, test_cost, place, scores)
        with jax.named_scope("sum_z"):
            scores = scores + unpack(lax.ppermute(pack(scores), "col", swap(2)))
            ratios = scores[:PAIR] / cost
            low_ratios = ratios.astype(bf16)
            if first:
                sums = [part.astype(bf16) for part in bf16_parts(scores[PAIR:])]
                low_ratios = jnp.concatenate([low_ratios] + sums, axis=0)
        with jax.named_scope("gather"):
            lows = [low_ratios] + [lax.ppermute(low_ratios, "col", ring(16, d, 4)) for d in (1, 2, 3)]
            low_here = jnp.concatenate(lows, axis=0)
            low_away = lax.ppermute(low_here, "col", swap(1))
            if first:
                sums_here, sums_away = low_here, low_away
        with jax.named_scope("total"):
            total = total_load(sums_here, sums_away, low_here, low_away)
            total = sum_four([total] + [lax.ppermute(total, "row", ring(4, d)) for d in (1, 2, 3)])
            row_total = total
            total = pair_sum(pair_sum(total, "depth", 1), "depth", 2)
        with jax.named_scope("loads"):
            load, size = half_loads(flipped_here, low_here)
            load = whole_loads(flipped_away, low_away, load, size)
            load = to_float16(jnp.concatenate([load[:-8], jnp.minimum(row_total, 1.0)], axis=0))
        with jax.named_scope("sum_y"):
            sent = load.astype(jnp.float16)
            wires = [load] + [lax.ppermute(sent, "row", ring(4, d)).astype(f32) for d in (1, 2, 3)]
        with jax.named_scope("update"):
            if iteration < ITERS - 1:
                current, low_weights = update(wires, total, current, place)
            else:
                current, primal = update(wires, total, current, place, ratios)
    return (current, primal)


def solution(mesh):
    placed = (P("row", "col"), P("row", "col"), P("col", "depth"), P("row", "depth"))
    return jax.shard_map(
        body,
        mesh=mesh,
        in_specs=placed,
        out_specs=(P("col", "depth"), P(("row", "col"), "depth")),
        check_vma=False,
    )
```

profile of v0, /device:TPU:8, one launch (start us, length us, event | category | flops | bytes accessed | tf_op | source)
XLA Modules:
  0.0 118.9 jit_solution(15343065285561027537)
XLA Ops:
  0.7 5.1 %scores.4 = (f32[1568,128]{1,0:T(8,128)S(1)}, bf16[8,2,192,1024]{3,2,1,0:T(8,128)(2,1)S(1)}, bf16[1024,128]{1,0:T(8,128)(2,1)S(1)}) custom-call(s32[4]{0:T(128)S(1)} %pad_add_fusion.place_ref, s32[8,24]{1,0:T(8,128)} %bitcast.15, bf16[8,2,192,1024]{3,2,1,0:T(8,128)(2,1)} %bitcast.14, bf16[1024,128]{1,0:T(8,128)(2,1)} %prior_ref.1), custom_call_target="tpu_custom_call" | custom-call | flops 402653184 | bytes 1006632 | tf_op jit(solution)/shard_map/scores/pallas_call | solution.py:112
  5.9 1.8 %scores.5 = f32[1568,128]{1,0:T(8,128)S(1)} custom-call(bf16[8,2,192,1024]{3,2,1,0:T(8,128)(2,1)S(1)} %get-tuple-element.14.kept_ref, bf16[1024,128]{1,0:T(8,128)(2,1)S(1)} %get-tuple-element.15.weights_ref.current_ref), custom_call_target="tpu_custom_call" | custom-call | flops 402653184 | bytes 1006632 | tf_op jit(solution)/shard_map/scores/pallas_call | solution.py:128
  8.5 3.1 %collective-permute-start.1 = (bf16[416,128]{1,0:T(8,128)(2,1)S(1)}, bf16[416,128]{1,0:T(8,128)(2,1)S(1)}, u32[]{:S(2)}, u32[]{:S(2)}) collective-permute-start(bf16[416,128]{1,0:T(8,128)(2,1)S(1)} %constant_dynamic-update-slice_fusion), channel_id=1, source_target_pairs={{0,32},{4,36},{8,40},{12,44},{16,48},{20,52},{24,56},{28,60},{32,0... | collective-permute-start | bytes 319496 | tf_op jit(solution)/shard_map/sum_x/ppermute | solution.py:373
  11.6 1.1 collective-permute-start.3
  12.7 0.9 collective-permute-start.2
  13.6 3.8 %collective-permute-done.3 = bf16[416,128]{1,0:T(8,128)(2,1)S(1)} collective-permute-done((bf16[416,128]{1,0:T(8,128)(2,1)S(1)}, bf16[416,128]{1,0:T(8,128)(2,1)S(1)}, u32[]{:S(2)}, u32[]{:S(2)}) %collective-permute-start.3) | collective-permute-done | bytes 106528 | tf_op jit(solution)/shard_map/sum_x/ppermute | solution.py:373
  17.5 1.2 collective-permute-done.2
  18.9 2.0 %collective-permute-start.4 = (bf16[416,128]{1,0:T(8,128)(2,1)S(1)}, bf16[416,128]{1,0:T(8,128)(2,1)S(1)}, u32[]{:S(2)}, u32[]{:S(2)}) collective-permute-start(bf16[416,128]{1,0:T(8,128)(2,1)S(1)} %constant_dynamic-update-slice_fusion.12), channel_id=1, source_target_pairs={{0,8},{4,12},{8,0},{12,4},{16,24},{20,28},{24,16},{28,20},{32,40},... | collective-permute-start | bytes 319496 | tf_op jit(solution)/shard_map/sum_z/ppermute | solution.py:379
  20.9 2.3 %flip.1 = (bf16[1024,1536]{1,0:T(8,128)(2,1)S(1)}, bf16[1024,1536]{1,0:T(8,128)(2,1)S(1)}, f32[384,128]{1,0:T(8,128)S(1)}) custom-call(s32[4]{0:T(128)S(1)} %pad_add_fusion.place_ref, bf16[8,2,192,1024]{3,2,1,0:T(8,128)(2,1)S(1)} %get-tuple-element.14.kept_ref, s32[3072,128]{1,0:T(8,128)} %cost_ref.1, f32[392,128]{1,0:T(8,128)S(1)} %fusion.4.after_ref), custom_call_target="tpu_custom_call" | custom-call | flops 3221225472 | bytes 8053063 | tf_op jit(solution)/shard_map/flip/pallas_call | solution.py:175
  23.9 1.8 %collective-permute-start.7 = (bf16[416,128]{1,0:T(8,128)(2,1)S(1)}, bf16[416,128]{1,0:T(8,128)(2,1)S(1)}, u32[]{:S(2)}, u32[]{:S(2)}) collective-permute-start(bf16[416,128]{1,0:T(8,128)(2,1)S(1)} %constant_dynamic-update-slice_fusion.16), channel_id=1, source_target_pairs={{0,48},{4,52},{8,56},{12,60},{16,0},{20,4},{24,8},{28,12},{32,16},... | collective-permute-start | bytes 319496 | tf_op jit(solution)/shard_map/gather/ppermute | solution.py:386
  25.7 0.9 collective-permute-start.6
  27.3 6.0 %collective-permute-done.5 = bf16[416,128]{1,0:T(8,128)(2,1)S(1)} collective-permute-done((bf16[416,128]{1,0:T(8,128)(2,1)S(1)}, bf16[416,128]{1,0:T(8,128)(2,1)S(1)}, u32[]{:S(2)}, u32[]{:S(2)}) %collective-permute-start.5) | collective-permute-done | bytes 106528 | tf_op jit(solution)/shard_map/gather/ppermute | solution.py:386
  33.7 1.1 loads.4
  36.4 1.6 %collective-permute-start.10 = (f32[8,128]{1,0:T(8,128)S(1)}, f32[8,128]{1,0:T(8,128)S(1)}, u32[]{:S(2)}, u32[]{:S(2)}) collective-permute-start(f32[8,128]{1,0:T(8,128)S(1)} %total.2), channel_id=1, source_target_pairs={{0,64},{64,128},{128,192},{192,0},{1,65},{65,129},{129,193},{193,1... | collective-permute-start | bytes 12296 | tf_op jit(solution)/shard_map/total/ppermute | solution.py:393
  38.0 3.5 %collective-permute-start.9 = (f32[8,128]{1,0:T(8,128)S(1)}, f32[8,128]{1,0:T(8,128)S(1)}, u32[]{:S(2)}, u32[]{:S(2)}) collective-permute-start(f32[8,128]{1,0:T(8,128)S(1)} %total.2), channel_id=1, source_target_pairs={{0,128},{64,192},{128,0},{192,64},{1,129},{65,193},{129,1},{193,65... | collective-permute-start | bytes 12296 | tf_op jit(solution)/shard_map/total/ppermute | solution.py:393
  41.5 1.1 loads.5
  43.4 1.5 %collective-permute-start.14 = (f16[1040,128]{1,0:T(8,128)(2,1)S(1)}, f16[1040,128]{1,0:T(8,128)(2,1)S(1)}, u32[]{:S(2)}, u32[]{:S(2)}) collective-permute-start(f16[1040,128]{1,0:T(8,128)(2,1)S(1)} %get-tuple-element.63), channel_id=1, source_target_pairs={{0,192},{64,0},{128,64},{192,128},{1,193},{65,1},{129,65},{193,129... | collective-permute-start | bytes 798728 | tf_op jit(solution)/shard_map/sum_y/ppermute | solution.py:402
  44.9 2.2 %collective-permute-start.13 = (f16[1040,128]{1,0:T(8,128)(2,1)S(1)}, f16[1040,128]{1,0:T(8,128)(2,1)S(1)}, u32[]{:S(2)}, u32[]{:S(2)}) collective-permute-start(f16[1040,128]{1,0:T(8,128)(2,1)S(1)} %get-tuple-element.63), channel_id=1, source_target_pairs={{0,128},{64,192},{128,0},{192,64},{1,129},{65,193},{129,1},{193,65... | collective-permute-start | bytes 798728 | tf_op jit(solution)/shard_map/sum_y/ppermute | solution.py:402
  47.1 2.5 %collective-permute-start.12 = (f16[1040,128]{1,0:T(8,128)(2,1)S(1)}, f16[1040,128]{1,0:T(8,128)(2,1)S(1)}, u32[]{:S(2)}, u32[]{:S(2)}) collective-permute-start(f16[1040,128]{1,0:T(8,128)(2,1)S(1)} %get-tuple-element.63), channel_id=1, source_target_pairs={{0,64},{64,128},{128,192},{192,0},{1,65},{65,129},{129,193},{193,1... | collective-permute-start | bytes 798728 | tf_op jit(solution)/shard_map/sum_y/ppermute | solution.py:402
  49.6 3.3 %collective-permute-start.15 = (f32[8,128]{1,0:T(8,128)S(1)}, f32[8,128]{1,0:T(8,128)S(1)}, u32[]{:S(2)}, u32[]{:S(2)}) collective-permute-start(f32[8,128]{1,0:T(8,128)S(1)} %get-tuple-element.44), channel_id=1, source_target_pairs={{0,1},{1,0},{2,3},{3,2},{4,5},{5,4},{6,7},{7,6},{8,9},{9,8},{10,11... | collective-permute-start | bytes 12296 | tf_op jit(solution)/shard_map/total/ppermute | solution.py:348
  52.9 1.6 %collective-permute-done.15 = f32[8,128]{1,0:T(8,128)S(1)} collective-permute-done((f32[8,128]{1,0:T(8,128)S(1)}, f32[8,128]{1,0:T(8,128)S(1)}, u32[]{:S(2)}, u32[]{:S(2)}) %collective-permute-start.15) | collective-permute-done | bytes 4128 | tf_op jit(solution)/shard_map/total/ppermute | solution.py:348
  54.5 6.5 %collective-permute-start.16 = (f32[8,128]{1,0:T(8,128)S(1)}, f32[8,128]{1,0:T(8,128)S(1)}, u32[]{:S(2)}, u32[]{:S(2)}) collective-permute-start(f32[8,128]{1,0:T(8,128)S(1)} %add.131), channel_id=1, source_target_pairs={{0,2},{1,3},{2,0},{3,1},{4,6},{5,7},{6,4},{7,5},{8,10},{9,11},{10,... | collective-permute-start | bytes 12296 | tf_op jit(solution)/shard_map/total/ppermute | solution.py:348
  60.9 1.6 %collective-permute-done.16 = f32[8,128]{1,0:T(8,128)S(1)} collective-permute-done((f32[8,128]{1,0:T(8,128)S(1)}, f32[8,128]{1,0:T(8,128)S(1)}, u32[]{:S(2)}, u32[]{:S(2)}) %collective-permute-start.16) | collective-permute-done | bytes 4128 | tf_op jit(solution)/shard_map/total/ppermute | solution.py:348
  63.5 1.0 scores.7
  64.5 1.0 scores.6
  65.5 1.3 %collective-permute-done.17 = f32[1536,128]{1,0:T(8,128)S(1)} collective-permute-done((f32[1536,128]{1,0:T(8,128)S(1)}, f32[1536,128]{1,0:T(8,128)S(1)}, u32[]{:S(2)}, u32[]{:S(2)}) %collective-permute-start.17) | collective-permute-done | bytes 786464 | tf_op jit(solution)/shard_map/scores/ppermute | solution.py:370
  67.3 3.3 %collective-permute-start.20 = (s16[400,128]{1,0:T(8,128)(2,1)S(1)}, s16[400,128]{1,0:T(8,128)(2,1)S(1)}, u32[]{:S(2)}, u32[]{:S(2)}) collective-permute-start(s16[400,128]{1,0:T(8,128)(2,1)S(1)} %fusion.2), channel_id=1, source_target_pairs={{0,48},{4,52},{8,56},{12,60},{16,0},{20,4},{24,8},{28,12},{32,16},... | collective-permute-start | bytes 307208 | tf_op jit(solution)/shard_map/sum_x/ppermute | solution.py:373
  70.9 2.4 %collective-permute-done.19 = s16[400,128]{1,0:T(8,128)(2,1)S(1)} collective-permute-done((s16[400,128]{1,0:T(8,128)(2,1)S(1)}, s16[400,128]{1,0:T(8,128)(2,1)S(1)}, u32[]{:S(2)}, u32[]{:S(2)}) %collective-permute-start.19) | collective-permute-done | bytes 102432 | tf_op jit(solution)/shard_map/sum_x/ppermute | solution.py:373
  73.4 1.5 %collective-permute-done.20 = s16[400,128]{1,0:T(8,128)(2,1)S(1)} collective-permute-done((s16[400,128]{1,0:T(8,128)(2,1)S(1)}, s16[400,128]{1,0:T(8,128)(2,1)S(1)}, u32[]{:S(2)}, u32[]{:S(2)}) %collective-permute-start.20) | collective-permute-done | bytes 102432 | tf_op jit(solution)/shard_map/sum_x/ppermute | solution.py:373
  75.0 2.1 %collective-permute-done.18 = s16[400,128]{1,0:T(8,128)(2,1)S(1)} collective-permute-done((s16[400,128]{1,0:T(8,128)(2,1)S(1)}, s16[400,128]{1,0:T(8,128)(2,1)S(1)}, u32[]{:S(2)}, u32[]{:S(2)}) %collective-permute-start.18) | collective-permute-done | bytes 102432 | tf_op jit(solution)/shard_map/sum_x/ppermute | solution.py:373
  77.3 1.1 collective-permute-start.21
  78.5 3.6 %collective-permute-done.21 = s16[400,128]{1,0:T(8,128)(2,1)S(1)} collective-permute-done((s16[400,128]{1,0:T(8,128)(2,1)S(1)}, s16[400,128]{1,0:T(8,128)(2,1)S(1)}, u32[]{:S(2)}, u32[]{:S(2)}) %collective-permute-start.21) | collective-permute-done | bytes 102432 | tf_op jit(solution)/shard_map/sum_z/ppermute | solution.py:379
  82.2 1.7 %collective-permute-start.24 = (bf16[384,128]{1,0:T(8,128)(2,1)S(1)}, bf16[384,128]{1,0:T(8,128)(2,1)S(1)}, u32[]{:S(2)}, u32[]{:S(2)}) collective-permute-start(bf16[384,128]{1,0:T(8,128)(2,1)S(1)} %get-tuple-element.31), channel_id=1, source_target_pairs={{0,48},{4,52},{8,56},{12,60},{16,0},{20,4},{24,8},{28,12},{32,16},... | collective-permute-start | bytes 294920 | tf_op jit(solution)/shard_map/gather/ppermute | solution.py:386
  83.9 1.0 collective-permute-start.22
  84.9 2.0 %collective-permute-done.24 = bf16[384,128]{1,0:T(8,128)(2,1)S(1)} collective-permute-done((bf16[384,128]{1,0:T(8,128)(2,1)S(1)}, bf16[384,128]{1,0:T(8,128)(2,1)S(1)}, u32[]{:S(2)}, u32[]{:S(2)}) %collective-permute-start.24) | collective-permute-done | bytes 98336 | tf_op jit(solution)/shard_map/gather/ppermute | solution.py:386
  86.9 3.2 %collective-permute-done.23 = bf16[384,128]{1,0:T(8,128)(2,1)S(1)} collective-permute-done((bf16[384,128]{1,0:T(8,128)(2,1)S(1)}, bf16[384,128]{1,0:T(8,128)(2,1)S(1)}, u32[]{:S(2)}, u32[]{:S(2)}) %collective-permute-start.23) | collective-permute-done | bytes 98336 | tf_op jit(solution)/shard_map/gather/ppermute | solution.py:386
  90.9 1.1 loads.6
  93.2 2.0 %collective-permute-start.27 = (f32[8,128]{1,0:T(8,128)S(1)}, f32[8,128]{1,0:T(8,128)S(1)}, u32[]{:S(2)}, u32[]{:S(2)}) collective-permute-start(f32[8,128]{1,0:T(8,128)S(1)} %total.3), channel_id=1, source_target_pairs={{0,64},{64,128},{128,192},{192,0},{1,65},{65,129},{129,193},{193,1... | collective-permute-start | bytes 12296 | tf_op jit(solution)/shard_map/total/ppermute | solution.py:393
  95.2 1.8 %collective-permute-start.26 = (f32[8,128]{1,0:T(8,128)S(1)}, f32[8,128]{1,0:T(8,128)S(1)}, u32[]{:S(2)}, u32[]{:S(2)}) collective-permute-start(f32[8,128]{1,0:T(8,128)S(1)} %total.3), channel_id=1, source_target_pairs={{0,128},{64,192},{128,0},{192,64},{1,129},{65,193},{129,1},{193,65... | collective-permute-start | bytes 12296 | tf_op jit(solution)/shard_map/total/ppermute | solution.py:393
  97.0 1.1 loads.7
  98.2 2.1 %collective-permute-done.26 = f32[8,128]{1,0:T(8,128)S(1)} collective-permute-done((f32[8,128]{1,0:T(8,128)S(1)}, f32[8,128]{1,0:T(8,128)S(1)}, u32[]{:S(2)}, u32[]{:S(2)}) %collective-permute-start.26) | collective-permute-done | bytes 4128 | tf_op jit(solution)/shard_map/total/ppermute | solution.py:393
  100.7 1.8 %collective-permute-start.30 = (f16[1040,128]{1,0:T(8,128)(2,1)S(1)}, f16[1040,128]{1,0:T(8,128)(2,1)S(1)}, u32[]{:S(2)}, u32[]{:S(2)}) collective-permute-start(f16[1040,128]{1,0:T(8,128)(2,1)S(1)} %get-tuple-element.61), channel_id=1, source_target_pairs={{0,128},{64,192},{128,0},{192,64},{1,129},{65,193},{129,1},{193,65... | collective-permute-start | bytes 798728 | tf_op jit(solution)/shard_map/sum_y/ppermute | solution.py:402
  102.6 2.5 %collective-permute-start.29 = (f16[1040,128]{1,0:T(8,128)(2,1)S(1)}, f16[1040,128]{1,0:T(8,128)(2,1)S(1)}, u32[]{:S(2)}, u32[]{:S(2)}) collective-permute-start(f16[1040,128]{1,0:T(8,128)(2,1)S(1)} %get-tuple-element.61), channel_id=1, source_target_pairs={{0,64},{64,128},{128,192},{192,0},{1,65},{65,129},{129,193},{193,1... | collective-permute-start | bytes 798728 | tf_op jit(solution)/shard_map/sum_y/ppermute | solution.py:402
  105.1 2.4 %collective-permute-start.32 = (f32[8,128]{1,0:T(8,128)S(1)}, f32[8,128]{1,0:T(8,128)S(1)}, u32[]{:S(2)}, u32[]{:S(2)}) collective-permute-start(f32[8,128]{1,0:T(8,128)S(1)} %get-tuple-element.30), channel_id=1, source_target_pairs={{0,1},{1,0},{2,3},{3,2},{4,5},{5,4},{6,7},{7,6},{8,9},{9,8},{10,11... | collective-permute-start | bytes 12296 | tf_op jit(solution)/shard_map/total/ppermute | solution.py:348
  107.5 2.1 %collective-permute-done.32 = f32[8,128]{1,0:T(8,128)S(1)} collective-permute-done((f32[8,128]{1,0:T(8,128)S(1)}, f32[8,128]{1,0:T(8,128)S(1)}, u32[]{:S(2)}, u32[]{:S(2)}) %collective-permute-start.32) | collective-permute-done | bytes 4128 | tf_op jit(solution)/shard_map/total/ppermute | solution.py:348
  109.6 5.9 %collective-permute-start.33 = (f32[8,128]{1,0:T(8,128)S(1)}, f32[8,128]{1,0:T(8,128)S(1)}, u32[]{:S(2)}, u32[]{:S(2)}) collective-permute-start(f32[8,128]{1,0:T(8,128)S(1)} %add.145), channel_id=1, source_target_pairs={{0,2},{1,3},{2,0},{3,1},{4,6},{5,7},{6,4},{7,5},{8,10},{9,11},{10,... | collective-permute-start | bytes 12296 | tf_op jit(solution)/shard_map/total/ppermute | solution.py:348
  115.5 1.6 %collective-permute-done.33 = f32[8,128]{1,0:T(8,128)S(1)} collective-permute-done((f32[8,128]{1,0:T(8,128)S(1)}, f32[8,128]{1,0:T(8,128)S(1)}, u32[]{:S(2)}, u32[]{:S(2)}) %collective-permute-start.33) | collective-permute-done | bytes 4128 | tf_op jit(solution)/shard_map/total/ppermute | solution.py:348
  117.3 1.6 %update.3 = (f32[1024,128]{1,0:T(8,128)}, f32[192,128]{1,0:T(8,128)}) custom-call(s32[4]{0:T(128)S(1)} %pad_add_fusion.place_ref, f32[1040,128]{1,0:T(8,128)S(1)} %get-tuple-element.62.zero, f32[1040,128]{1,0:T(8,128)S(1)} %convert_element_type.134.one, f32[1040,128]{1,0:T(8,128)S(1)} %convert_element_type.135.two, ...), custom_call_target="tpu_custom_call" | custom-call | flops 10000000 | bytes 25000 | tf_op jit(solution)/shard_map/update/pallas_call | solution.py:330
  (113 shorter events, 9.9 us)
Async XLA Ops:
  5.8 2.4 %collective-permute-start = (f32[1568,128]{1,0:T(8,128)S(1)}, f32[1568,128]{1,0:T(8,128)S(1)}, u32[]{:S(2)}, u32[]{:S(2)}) collective-permute-start(f32[1568,128]{1,0:T(8,128)S(1)} %get-tuple-element.16), channel_id=1, source_target_pairs={{0,4},{4,0},{8,12},{12,8},{16,20},{20,16},{24,28},{28,24},{32,36},... | collective-permute-start | bytes 2408456 | tf_op jit(solution)/shard_map/scores/ppermute | solution.py:370
  8.5 10.2 %collective-permute-start.1 = (bf16[416,128]{1,0:T(8,128)(2,1)S(1)}, bf16[416,128]{1,0:T(8,128)(2,1)S(1)}, u32[]{:S(2)}, u32[]{:S(2)}) collective-permute-start(bf16[416,128]{1,0:T(8,128)(2,1)S(1)} %constant_dynamic-update-slice_fusion), channel_id=1, source_target_pairs={{0,32},{4,36},{8,40},{12,44},{16,48},{20,52},{24,56},{28,60},{32,0... | collective-permute-start | bytes 319496 | tf_op jit(solution)/shard_map/sum_x/ppermute | solution.py:373
  11.6 5.9 %collective-permute-start.3 = (bf16[416,128]{1,0:T(8,128)(2,1)S(1)}, bf16[416,128]{1,0:T(8,128)(2,1)S(1)}, u32[]{:S(2)}, u32[]{:S(2)}) collective-permute-start(bf16[416,128]{1,0:T(8,128)(2,1)S(1)} %constant_dynamic-update-slice_fusion.8), channel_id=1, source_target_pairs={{0,48},{4,52},{8,56},{12,60},{16,0},{20,4},{24,8},{28,12},{32,16},... | collective-permute-start | bytes 319496 | tf_op jit(solution)/shard_map/sum_x/ppermute | solution.py:373
  12.7 5.9 %collective-permute-start.2 = (bf16[416,128]{1,0:T(8,128)(2,1)S(1)}, bf16[416,128]{1,0:T(8,128)(2,1)S(1)}, u32[]{:S(2)}, u32[]{:S(2)}) collective-permute-start(bf16[416,128]{1,0:T(8,128)(2,1)S(1)} %constant_dynamic-update-slice_fusion.4), channel_id=1, source_target_pairs={{0,16},{4,20},{8,24},{12,28},{16,32},{20,36},{24,40},{28,44},{32,4... | collective-permute-start | bytes 319496 | tf_op jit(solution)/shard_map/sum_x/ppermute | solution.py:373
  18.9 4.8 %collective-permute-start.4 = (bf16[416,128]{1,0:T(8,128)(2,1)S(1)}, bf16[416,128]{1,0:T(8,128)(2,1)S(1)}, u32[]{:S(2)}, u32[]{:S(2)}) collective-permute-start(bf16[416,128]{1,0:T(8,128)(2,1)S(1)} %constant_dynamic-update-slice_fusion.12), channel_id=1, source_target_pairs={{0,8},{4,12},{8,0},{12,4},{16,24},{20,28},{24,16},{28,20},{32,40},... | collective-permute-start | bytes 319496 | tf_op jit(solution)/shard_map/sum_z/ppermute | solution.py:379
  23.9 9.5 %collective-permute-start.7 = (bf16[416,128]{1,0:T(8,128)(2,1)S(1)}, bf16[416,128]{1,0:T(8,128)(2,1)S(1)}, u32[]{:S(2)}, u32[]{:S(2)}) collective-permute-start(bf16[416,128]{1,0:T(8,128)(2,1)S(1)} %constant_dynamic-update-slice_fusion.16), channel_id=1, source_target_pairs={{0,48},{4,52},{8,56},{12,60},{16,0},{20,4},{24,8},{28,12},{32,16},... | collective-permute-start | bytes 319496 | tf_op jit(solution)/shard_map/gather/ppermute | solution.py:386
  25.7 7.6 %collective-permute-start.6 = (bf16[416,128]{1,0:T(8,128)(2,1)S(1)}, bf16[416,128]{1,0:T(8,128)(2,1)S(1)}, u32[]{:S(2)}, u32[]{:S(2)}) collective-permute-start(bf16[416,128]{1,0:T(8,128)(2,1)S(1)} %constant_dynamic-update-slice_fusion.16), channel_id=1, source_target_pairs={{0,32},{4,36},{8,40},{12,44},{16,48},{20,52},{24,56},{28,60},{32,0... | collective-permute-start | bytes 319496 | tf_op jit(solution)/shard_map/gather/ppermute | solution.py:386
  26.7 6.7 %collective-permute-start.5 = (bf16[416,128]{1,0:T(8,128)(2,1)S(1)}, bf16[416,128]{1,0:T(8,128)(2,1)S(1)}, u32[]{:S(2)}, u32[]{:S(2)}) collective-permute-start(bf16[416,128]{1,0:T(8,128)(2,1)S(1)} %constant_dynamic-update-slice_fusion.16), channel_id=1, source_target_pairs={{0,16},{4,20},{8,24},{12,28},{16,32},{20,36},{24,40},{28,44},{32,4... | collective-permute-start | bytes 319496 | tf_op jit(solution)/shard_map/gather/ppermute | solution.py:386
  33.4 2.0 %collective-permute-start.8 = (bf16[1664,128]{1,0:T(8,128)(2,1)S(1)}, bf16[1664,128]{1,0:T(8,128)(2,1)S(1)}, u32[]{:S(2)}, u32[]{:S(2)}) collective-permute-start(bf16[1664,128]{1,0:T(8,128)(2,1)S(1)} %constant_dynamic-update-slice_fusion.21.low_ref.sums_own.low_own), channel_id=1, source_target_pairs={{0,4},{4,0},{8,12},{12,8},{16,20},{20,16},{24,28},{28,24},{32,36},... | collective-permute-start | bytes 1277960 | tf_op jit(solution)/shard_map/gather/ppermute | solution.py:388
  35.9 6.8 %collective-permute-start.11 = (f32[8,128]{1,0:T(8,128)S(1)}, f32[8,128]{1,0:T(8,128)S(1)}, u32[]{:S(2)}, u32[]{:S(2)}) collective-permute-start(f32[8,128]{1,0:T(8,128)S(1)} %total.2), channel_id=1, source_target_pairs={{0,192},{64,0},{128,64},{192,128},{1,193},{65,1},{129,65},{193,129... | collective-permute-start | bytes 12296 | tf_op jit(solution)/shard_map/total/ppermute | solution.py:393
  36.4 6.3 %collective-permute-start.10 = (f32[8,128]{1,0:T(8,128)S(1)}, f32[8,128]{1,0:T(8,128)S(1)}, u32[]{:S(2)}, u32[]{:S(2)}) collective-permute-start(f32[8,128]{1,0:T(8,128)S(1)} %total.2), channel_id=1, source_target_pairs={{0,64},{64,128},{128,192},{192,0},{1,65},{65,129},{129,193},{193,1... | collective-permute-start | bytes 12296 | tf_op jit(solution)/shard_map/total/ppermute | solution.py:393
  38.0 5.1 %collective-permute-start.9 = (f32[8,128]{1,0:T(8,128)S(1)}, f32[8,128]{1,0:T(8,128)S(1)}, u32[]{:S(2)}, u32[]{:S(2)}) collective-permute-start(f32[8,128]{1,0:T(8,128)S(1)} %total.2), channel_id=1, source_target_pairs={{0,128},{64,192},{128,0},{192,64},{1,129},{65,193},{129,1},{193,65... | collective-permute-start | bytes 12296 | tf_op jit(solution)/shard_map/total/ppermute | solution.py:393
  43.4 19.1 %collective-permute-start.14 = (f16[1040,128]{1,0:T(8,128)(2,1)S(1)}, f16[1040,128]{1,0:T(8,128)(2,1)S(1)}, u32[]{:S(2)}, u32[]{:S(2)}) collective-permute-start(f16[1040,128]{1,0:T(8,128)(2,1)S(1)} %get-tuple-element.63), channel_id=1, source_target_pairs={{0,192},{64,0},{128,64},{192,128},{1,193},{65,1},{129,65},{193,129... | collective-permute-start | bytes 798728 | tf_op jit(solution)/shard_map/sum_y/ppermute | solution.py:402
  44.9 17.7 %collective-permute-start.13 = (f16[1040,128]{1,0:T(8,128)(2,1)S(1)}, f16[1040,128]{1,0:T(8,128)(2,1)S(1)}, u32[]{:S(2)}, u32[]{:S(2)}) collective-permute-start(f16[1040,128]{1,0:T(8,128)(2,1)S(1)} %get-tuple-element.63), channel_id=1, source_target_pairs={{0,128},{64,192},{128,0},{192,64},{1,129},{65,193},{129,1},{193,65... | collective-permute-start | bytes 798728 | tf_op jit(solution)/shard_map/sum_y/ppermute | solution.py:402
  47.1 15.5 %collective-permute-start.12 = (f16[1040,128]{1,0:T(8,128)(2,1)S(1)}, f16[1040,128]{1,0:T(8,128)(2,1)S(1)}, u32[]{:S(2)}, u32[]{:S(2)}) collective-permute-start(f16[1040,128]{1,0:T(8,128)(2,1)S(1)} %get-tuple-element.63), channel_id=1, source_target_pairs={{0,64},{64,128},{128,192},{192,0},{1,65},{65,129},{129,193},{193,1... | collective-permute-start | bytes 798728 | tf_op jit(solution)/shard_map/sum_y/ppermute | solution.py:402
  49.6 4.9 %collective-permute-start.15 = (f32[8,128]{1,0:T(8,128)S(1)}, f32[8,128]{1,0:T(8,128)S(1)}, u32[]{:S(2)}, u32[]{:S(2)}) collective-permute-start(f32[8,128]{1,0:T(8,128)S(1)} %get-tuple-element.44), channel_id=1, source_target_pairs={{0,1},{1,0},{2,3},{3,2},{4,5},{5,4},{6,7},{7,6},{8,9},{9,8},{10,11... | collective-permute-start | bytes 12296 | tf_op jit(solution)/shard_map/total/ppermute | solution.py:348
  54.5 8.1 %collective-permute-start.16 = (f32[8,128]{1,0:T(8,128)S(1)}, f32[8,128]{1,0:T(8,128)S(1)}, u32[]{:S(2)}, u32[]{:S(2)}) collective-permute-start(f32[8,128]{1,0:T(8,128)S(1)} %add.131), channel_id=1, source_target_pairs={{0,2},{1,3},{2,0},{3,1},{4,6},{5,7},{6,4},{7,5},{8,10},{9,11},{10,... | collective-permute-start | bytes 12296 | tf_op jit(solution)/shard_map/total/ppermute | solution.py:348
  64.4 2.4 %collective-permute-start.17 = (f32[1536,128]{1,0:T(8,128)S(1)}, f32[1536,128]{1,0:T(8,128)S(1)}, u32[]{:S(2)}, u32[]{:S(2)}) collective-permute-start(f32[1536,128]{1,0:T(8,128)S(1)} %scores.7), channel_id=1, source_target_pairs={{0,4},{4,0},{8,12},{12,8},{16,20},{20,16},{24,28},{28,24},{32,36},... | collective-permute-start | bytes 2359304 | tf_op jit(solution)/shard_map/scores/ppermute | solution.py:370
  67.2 6.2 %collective-permute-start.19 = (s16[400,128]{1,0:T(8,128)(2,1)S(1)}, s16[400,128]{1,0:T(8,128)(2,1)S(1)}, u32[]{:S(2)}, u32[]{:S(2)}) collective-permute-start(s16[400,128]{1,0:T(8,128)(2,1)S(1)} %fusion.1), channel_id=1, source_target_pairs={{0,16},{4,20},{8,24},{12,28},{16,32},{20,36},{24,40},{28,44},{32,4... | collective-permute-start | bytes 307208 | tf_op jit(solution)/shard_map/sum_x/ppermute | solution.py:373
  67.3 7.6 %collective-permute-start.20 = (s16[400,128]{1,0:T(8,128)(2,1)S(1)}, s16[400,128]{1,0:T(8,128)(2,1)S(1)}, u32[]{:S(2)}, u32[]{:S(2)}) collective-permute-start(s16[400,128]{1,0:T(8,128)(2,1)S(1)} %fusion.2), channel_id=1, source_target_pairs={{0,48},{4,52},{8,56},{12,60},{16,0},{20,4},{24,8},{28,12},{32,16},... | collective-permute-start | bytes 307208 | tf_op jit(solution)/shard_map/sum_x/ppermute | solution.py:373
  70.6 6.5 %collective-permute-start.18 = (s16[400,128]{1,0:T(8,128)(2,1)S(1)}, s16[400,128]{1,0:T(8,128)(2,1)S(1)}, u32[]{:S(2)}, u32[]{:S(2)}) collective-permute-start(s16[400,128]{1,0:T(8,128)(2,1)S(1)} %fusion), channel_id=1, source_target_pairs={{0,32},{4,36},{8,40},{12,44},{16,48},{20,52},{24,56},{28,60},{32,0... | collective-permute-start | bytes 307208 | tf_op jit(solution)/shard_map/sum_x/ppermute | solution.py:373
  77.3 4.7 %collective-permute-start.21 = (s16[400,128]{1,0:T(8,128)(2,1)S(1)}, s16[400,128]{1,0:T(8,128)(2,1)S(1)}, u32[]{:S(2)}, u32[]{:S(2)}) collective-permute-start(s16[400,128]{1,0:T(8,128)(2,1)S(1)} %fusion.3), channel_id=1, source_target_pairs={{0,8},{4,12},{8,0},{12,4},{16,24},{20,28},{24,16},{28,20},{32,40},... | collective-permute-start | bytes 307208 | tf_op jit(solution)/shard_map/sum_z/ppermute | solution.py:379
  82.2 4.7 %collective-permute-start.24 = (bf16[384,128]{1,0:T(8,128)(2,1)S(1)}, bf16[384,128]{1,0:T(8,128)(2,1)S(1)}, u32[]{:S(2)}, u32[]{:S(2)}) collective-permute-start(bf16[384,128]{1,0:T(8,128)(2,1)S(1)} %get-tuple-element.31), channel_id=1, source_target_pairs={{0,48},{4,52},{8,56},{12,60},{16,0},{20,4},{24,8},{28,12},{32,16},... | collective-permute-start | bytes 294920 | tf_op jit(solution)/shard_map/gather/ppermute | solution.py:386
  83.9 6.2 %collective-permute-start.23 = (bf16[384,128]{1,0:T(8,128)(2,1)S(1)}, bf16[384,128]{1,0:T(8,128)(2,1)S(1)}, u32[]{:S(2)}, u32[]{:S(2)}) collective-permute-start(bf16[384,128]{1,0:T(8,128)(2,1)S(1)} %get-tuple-element.31), channel_id=1, source_target_pairs={{0,32},{4,36},{8,40},{12,44},{16,48},{20,52},{24,56},{28,60},{32,0... | collective-permute-start | bytes 294920 | tf_op jit(solution)/shard_map/gather/ppermute | solution.py:386
  83.9 6.9 %collective-permute-start.22 = (bf16[384,128]{1,0:T(8,128)(2,1)S(1)}, bf16[384,128]{1,0:T(8,128)(2,1)S(1)}, u32[]{:S(2)}, u32[]{:S(2)}) collective-permute-start(bf16[384,128]{1,0:T(8,128)(2,1)S(1)} %get-tuple-element.31), channel_id=1, source_target_pairs={{0,16},{4,20},{8,24},{12,28},{16,32},{20,36},{24,40},{28,44},{32,4... | collective-permute-start | bytes 294920 | tf_op jit(solution)/shard_map/gather/ppermute | solution.py:386
  90.8 1.8 %collective-permute-start.25 = (bf16[1536,128]{1,0:T(8,128)(2,1)S(1)}, bf16[1536,128]{1,0:T(8,128)(2,1)S(1)}, u32[]{:S(2)}, u32[]{:S(2)}) collective-permute-start(bf16[1536,128]{1,0:T(8,128)(2,1)S(1)} %pad_maximum_fusion.low_ref.low_own), channel_id=1, source_target_pairs={{0,4},{4,0},{8,12},{12,8},{16,20},{20,16},{24,28},{28,24},{32,36},... | collective-permute-start | bytes 1179656 | tf_op jit(solution)/shard_map/gather/ppermute | solution.py:388
  93.1 5.1 %collective-permute-start.28 = (f32[8,128]{1,0:T(8,128)S(1)}, f32[8,128]{1,0:T(8,128)S(1)}, u32[]{:S(2)}, u32[]{:S(2)}) collective-permute-start(f32[8,128]{1,0:T(8,128)S(1)} %total.3), channel_id=1, source_target_pairs={{0,192},{64,0},{128,64},{192,128},{1,193},{65,1},{129,65},{193,129... | collective-permute-start | bytes 12296 | tf_op jit(solution)/shard_map/total/ppermute | solution.py:393
  93.2 5.0 %collective-permute-start.27 = (f32[8,128]{1,0:T(8,128)S(1)}, f32[8,128]{1,0:T(8,128)S(1)}, u32[]{:S(2)}, u32[]{:S(2)}) collective-permute-start(f32[8,128]{1,0:T(8,128)S(1)} %total.3), channel_id=1, source_target_pairs={{0,64},{64,128},{128,192},{192,0},{1,65},{65,129},{129,193},{193,1... | collective-permute-start | bytes 12296 | tf_op jit(solution)/shard_map/total/ppermute | solution.py:393
  95.2 5.1 %collective-permute-start.26 = (f32[8,128]{1,0:T(8,128)S(1)}, f32[8,128]{1,0:T(8,128)S(1)}, u32[]{:S(2)}, u32[]{:S(2)}) collective-permute-start(f32[8,128]{1,0:T(8,128)S(1)} %total.3), channel_id=1, source_target_pairs={{0,128},{64,192},{128,0},{192,64},{1,129},{65,193},{129,1},{193,65... | collective-permute-start | bytes 12296 | tf_op jit(solution)/shard_map/total/ppermute | solution.py:393
  100.6 16.6 %collective-permute-start.31 = (f16[1040,128]{1,0:T(8,128)(2,1)S(1)}, f16[1040,128]{1,0:T(8,128)(2,1)S(1)}, u32[]{:S(2)}, u32[]{:S(2)}) collective-permute-start(f16[1040,128]{1,0:T(8,128)(2,1)S(1)} %get-tuple-element.61), channel_id=1, source_target_pairs={{0,192},{64,0},{128,64},{192,128},{1,193},{65,1},{129,65},{193,129... | collective-permute-start | bytes 798728 | tf_op jit(solution)/shard_map/sum_y/ppermute | solution.py:402
  100.7 16.4 %collective-permute-start.30 = (f16[1040,128]{1,0:T(8,128)(2,1)S(1)}, f16[1040,128]{1,0:T(8,128)(2,1)S(1)}, u32[]{:S(2)}, u32[]{:S(2)}) collective-permute-start(f16[1040,128]{1,0:T(8,128)(2,1)S(1)} %get-tuple-element.61), channel_id=1, source_target_pairs={{0,128},{64,192},{128,0},{192,64},{1,129},{65,193},{129,1},{193,65... | collective-permute-start | bytes 798728 | tf_op jit(solution)/shard_map/sum_y/ppermute | solution.py:402
  102.6 14.7 %collective-permute-start.29 = (f16[1040,128]{1,0:T(8,128)(2,1)S(1)}, f16[1040,128]{1,0:T(8,128)(2,1)S(1)}, u32[]{:S(2)}, u32[]{:S(2)}) collective-permute-start(f16[1040,128]{1,0:T(8,128)(2,1)S(1)} %get-tuple-element.61), channel_id=1, source_target_pairs={{0,64},{64,128},{128,192},{192,0},{1,65},{65,129},{129,193},{193,1... | collective-permute-start | bytes 798728 | tf_op jit(solution)/shard_map/sum_y/ppermute | solution.py:402
  105.1 4.5 %collective-permute-start.32 = (f32[8,128]{1,0:T(8,128)S(1)}, f32[8,128]{1,0:T(8,128)S(1)}, u32[]{:S(2)}, u32[]{:S(2)}) collective-permute-start(f32[8,128]{1,0:T(8,128)S(1)} %get-tuple-element.30), channel_id=1, source_target_pairs={{0,1},{1,0},{2,3},{3,2},{4,5},{5,4},{6,7},{7,6},{8,9},{9,8},{10,11... | collective-permute-start | bytes 12296 | tf_op jit(solution)/shard_map/total/ppermute | solution.py:348
  109.6 7.5 %collective-permute-start.33 = (f32[8,128]{1,0:T(8,128)S(1)}, f32[8,128]{1,0:T(8,128)S(1)}, u32[]{:S(2)}, u32[]{:S(2)}) collective-permute-start(f32[8,128]{1,0:T(8,128)S(1)} %add.145), channel_id=1, source_target_pairs={{0,2},{1,3},{2,0},{3,1},{4,6},{5,7},{6,4},{7,5},{8,10},{9,11},{10,... | collective-permute-start | bytes 12296 | tf_op jit(solution)/shard_map/total/ppermute | solution.py:348
where the time goes:
time: 119 us
  starting transfers between devices  56.9 us (48%)
  waiting for transfers between devices  39.7 us (33%)
  Pallas kernels  18.6 us (16%)
  other arithmetic  2.1 us (2%)
  between operations  1.28 us (1%)
    ppermute x4, starting transfers between devices, pair_sum(): return value + lax.ppermute(value, axis, [(i, i ^ bit) for i in range(4)])  18.1 us
    ppermute x6, waiting for transfers between devices, body(): lax.ppermute(low_ratios, 'col', ring(16, d, 4))  11.9 us
    ppermute x6, waiting for transfers between devices, body(): lax.ppermute(pack(here[d]), 'col', ring(16, d, 4))  11.1 us
    ppermute x6, starting transfers between devices, body(): lax.ppermute(sent, 'row', ring(4, d)).astype(f32)  10.7 us
    ppermute x6, starting transfers between devices, body(): lax.ppermute(total, 'row', ring(4, d))  9.53 us
    ppermute x6, starting transfers between devices, body(): lax.ppermute(pack(here[d]), 'col', ring(16, d, 4))  8.82 us
    ppermute x4, waiting for transfers between devices, pair_sum(): return value + lax.ppermute(value, axis, [(i, i ^ bit) for i in range(4)])  6.86 us
    ppermute x6, starting transfers between devices, body(): lax.ppermute(low_ratios, 'col', ring(16, d, 4))  6.08 us
  transfers between devices with their start and end apart: 34, of which 21 were waited for; matrix products, arithmetic and copies ran while one was open for 0% of the time, Pallas kernels for 8%

commit v1 on v0

--- a/solution.py
+++ b/solution.py
@@ -64,16 +64,13 @@
 def first_scores_kernel(place_ref, mask_ref, cover_ref, prior_ref, out_ref, kept_ref, weights_ref, rows_ref, tiles_ref, sems):
     tiles = pltpu.make_async_copy(mask_ref, tiles_ref, sems.at[8])
     tiles.start()
-    copies = {}
     for half in (1, 0):
         core = 1 - place_ref[1] if half else place_ref[1]
         for d in range(4):
             x = lax.rem(place_ref[0] + d, 4)
-            copy = pltpu.make_async_copy(
+            pltpu.make_async_copy(
                 cover_ref.at[pl.ds(2 * x, 2), core], kept_ref.at[half * 4 + d], sems.at[half * 4 + d]
-            )
-            copy.start()
-            copies[half, d] = copy
+            ).start()
         if half:
             weights = pltpu.make_async_copy(prior_ref, weights_ref, sems.at[9])
             weights.start()
@@ -86,20 +83,28 @@
     )
     weights.wait()
     lines = BLOCK // 2
-    for half in (1, 0):
-        core = 1 - place_ref[1] if half else place_ref[1]
-        for d in range(4):
-            copies[half, d].wait()
-            for z in range(2):
-                chunk = lax.rem(place_ref[0] + d, 4) * 4 + z * 2 + core
-                for j in range(CHUNK // lines):
-                    block_row = (chunk * (CHUNK // lines) + j) // 2
-                    entry = jnp.broadcast_to(rows_ref[pl.ds(block_row, 1), :], (16, edges)).astype(bf16)
-                    for k in range(lines // 16):
-                        at = slice(j * lines + k * 16, j * lines + k * 16 + 16)
-                        kept_ref[half * 4 + d, z, at, :] = kept_ref[half * 4 + d, z, at, :] * entry
-            if half:
-                scores_and_sums(tests_of(kept_ref, d, half), weights_ref[...], out_ref, d)
+
+    def arrive(half, core, d):
+        x = lax.rem(place_ref[0] + d, 4)
+        slot = half * 4 + d
+        pltpu.make_async_copy(cover_ref.at[pl.ds(2 * x, 2), core], kept_ref.at[slot], sems.at[slot]).wait()
+        for z in range(2):
+            for j in range(CHUNK // lines):
+                block_row = ((x * 4 + z * 2 + core) * (CHUNK // lines) + j) // 2
+                entry = jnp.broadcast_to(rows_ref[pl.ds(block_row, 1), :], (16, edges)).astype(bf16)
+                for k in range(lines // 16):
+                    at = slice(j * lines + k * 16, j * lines + k * 16 + 16)
+                    kept_ref[slot, z, at, :] = kept_ref[slot, z, at, :] * entry
+
+    for d in range(4):
+        arrive(1, 1 - place_ref[1], d)
+        scores_and_sums(tests_of(kept_ref, d, 1), weights_ref[...], out_ref, d)
+
+    def own(d, carry):
+        arrive(0, place_ref[1], d)
+        return carry
+
+    lax.fori_loop(0, 4, own, 0)
 
 
 def own_scores_kernel(kept_ref, weights_ref, out_ref):
@@ -163,8 +168,13 @@
         copy.start()
         copies.append(copy)
     for half, out_ref in enumerate((own_out, other_out)):
-        for d in range(4):
-            out_ref[:, d * PAIR : (d + 1) * PAIR] = tests_of(kept_ref, (4 - d) % 4, half).T
+
+        def step(d, carry, half=half, out_ref=out_ref):
+            columns = pl.ds(pl.multiple_of(d * PAIR, BLOCK), PAIR)
+            out_ref[:, columns] = tests_of(kept_ref, lax.rem(4 - d, 4), half).T
+            return carry
+
+        lax.fori_loop(0, 4, step, 0)
     for copy in copies:
         copy.wait()
     cost_out[...] = cost_in[...].astype(f32)
@@ -344,8 +354,8 @@
     return [(i, i ^ bit) for i in range(16)]
 
 
-def pair_sum(value, axis, bit):
-    return value + lax.ppermute(value, axis, [(i, i ^ bit) for i in range(4)])
+def sum_ring(value, axis):
+    return sum_four([value] + [lax.ppermute(value, axis, ring(4, d)) for d in (1, 2, 3)])
 
 
 def sum_four(parts):
@@ -390,9 +400,8 @@
                 sums_here, sums_away = low_here, low_away
         with jax.named_scope("total"):
             total = total_load(sums_here, sums_away, low_here, low_away)
-            total = sum_four([total] + [lax.ppermute(total, "row", ring(4, d)) for d in (1, 2, 3)])
-            row_total = total
-            total = pair_sum(pair_sum(total, "depth", 1), "depth", 2)
+            total = row_total = sum_ring(total, "row")
+            total = sum_ring(total, "depth")
         with jax.named_scope("loads"):
             load, size = half_loads(flipped_here, low_here)
             load = whole_loads(flipped_away, low_away, load, size)

time: 119 us -> 119 us (level); the launches traced: 119 us -> 118 us
  waiting for transfers between devices: 39.7 us -> 36.2 us
  starting transfers between devices: 56.9 us -> 58.8 us
    ppermute x10 -> x12, waiting for transfers between devices: 9.38 us -> 6.2 us  [sum_ring(): lax.ppermute(value, axis, ring(4, d))]
    ppermute x10 -> x12, starting transfers between devices: 27.6 us -> 29.5 us  [sum_ring(): lax.ppermute(value, axis, ring(4, d))]
  transfers between devices with their start and end apart: 34 -> 36, of which waited for: 21 -> 20; matrix products, arithmetic and copies ran while one was open for 0% -> 0% of each run, Pallas kernels for 8% -> 8%
where the time goes in v1:
time: 119 us; the launch traced here: 118 us
  starting transfers between devices  58.8 us (49%)
  waiting for transfers between devices  36.2 us (30%)
  Pallas kernels  19 us (16%)
  other arithmetic  2.1 us (2%)
  between operations  1.29 us (1%)
    ppermute x12, starting transfers between devices, sum_ring(): lax.ppermute(value, axis, ring(4, d))  29.5 us
    ppermute x6, waiting for transfers between devices, body(): lax.ppermute(low_ratios, 'col', ring(16, d, 4))  12 us
    ppermute x6, waiting for transfers between devices, body(): lax.ppermute(pack(here[d]), 'col', ring(16, d, 4))  11.1 us
    ppermute x6, starting transfers between devices, body(): lax.ppermute(sent, 'row', ring(4, d)).astype(f32)  10.7 us
    ppermute x6, starting transfers between devices, body(): lax.ppermute(pack(here[d]), 'col', ring(16, d, 4))  8.6 us
    ppermute x6, starting transfers between devices, body(): lax.ppermute(low_ratios, 'col', ring(16, d, 4))  6.52 us
    ppermute x12, waiting for transfers between devices, sum_ring(): lax.ppermute(value, axis, ring(4, d))  6.2 us
    pallas_call x1, Pallas kernels, first_scores(): call(first_scores_kernel, [pltpu.VMEM((4 * WITH_SUMS, scen), f32), pltpu....  5.09 us
  transfers between devices with their start and end apart: 36, of which 20 were waited for; matrix products, arithmetic and copies ran while one was open for 0% of the time, Pallas kernels for 8%

profile of v1, /device:TPU:8, one launch (start us, length us, event | category | flops | bytes accessed | tf_op | source)
XLA Modules:
  0.0 117.7 jit_solution(10996132369089197300)
XLA Ops:
  0.7 5.1 %scores.4 = (f32[1568,128]{1,0:T(8,128)S(1)}, bf16[8,2,192,1024]{3,2,1,0:T(8,128)(2,1)S(1)}, bf16[1024,128]{1,0:T(8,128)(2,1)S(1)}) custom-call(s32[4]{0:T(128)S(1)} %pad_add_fusion.place_ref, s32[8,24]{1,0:T(8,128)} %bitcast.15, bf16[8,2,192,1024]{3,2,1,0:T(8,128)(2,1)} %bitcast.14, bf16[1024,128]{1,0:T(8,128)(2,1)} %prior_ref.1), custom_call_target="tpu_custom_call" | custom-call | flops 402653184 | bytes 1006632 | tf_op jit(solution)/shard_map/scores/pallas_call | solution.py:117
  5.9 1.8 %scores.5 = f32[1568,128]{1,0:T(8,128)S(1)} custom-call(bf16[8,2,192,1024]{3,2,1,0:T(8,128)(2,1)S(1)} %get-tuple-element.14.kept_ref, bf16[1024,128]{1,0:T(8,128)(2,1)S(1)} %get-tuple-element.15.weights_ref.current_ref), custom_call_target="tpu_custom_call" | custom-call | flops 402653184 | bytes 1006632 | tf_op jit(solution)/shard_map/scores/pallas_call | solution.py:133
  8.4 3.1 %collective-permute-start.1 = (bf16[416,128]{1,0:T(8,128)(2,1)S(1)}, bf16[416,128]{1,0:T(8,128)(2,1)S(1)}, u32[]{:S(2)}, u32[]{:S(2)}) collective-permute-start(bf16[416,128]{1,0:T(8,128)(2,1)S(1)} %constant_dynamic-update-slice_fusion), channel_id=1, source_target_pairs={{0,32},{4,36},{8,40},{12,44},{16,48},{20,52},{24,56},{28,60},{32,0... | collective-permute-start | bytes 319496 | tf_op jit(solution)/shard_map/sum_x/ppermute | solution.py:383
  11.6 1.1 collective-permute-start.3
  12.7 0.9 collective-permute-start.2
  13.6 3.8 %collective-permute-done.3 = bf16[416,128]{1,0:T(8,128)(2,1)S(1)} collective-permute-done((bf16[416,128]{1,0:T(8,128)(2,1)S(1)}, bf16[416,128]{1,0:T(8,128)(2,1)S(1)}, u32[]{:S(2)}, u32[]{:S(2)}) %collective-permute-start.3) | collective-permute-done | bytes 106528 | tf_op jit(solution)/shard_map/sum_x/ppermute | solution.py:383
  17.4 1.2 collective-permute-done.2
  18.9 2.0 %collective-permute-start.4 = (bf16[416,128]{1,0:T(8,128)(2,1)S(1)}, bf16[416,128]{1,0:T(8,128)(2,1)S(1)}, u32[]{:S(2)}, u32[]{:S(2)}) collective-permute-start(bf16[416,128]{1,0:T(8,128)(2,1)S(1)} %constant_dynamic-update-slice_fusion.12), channel_id=1, source_target_pairs={{0,8},{4,12},{8,0},{12,4},{16,24},{20,28},{24,16},{28,20},{32,40},... | collective-permute-start | bytes 319496 | tf_op jit(solution)/shard_map/sum_z/ppermute | solution.py:389
  20.9 2.7 %flip.1 = (bf16[1024,1536]{1,0:T(8,128)(2,1)S(1)}, bf16[1024,1536]{1,0:T(8,128)(2,1)S(1)}, f32[384,128]{1,0:T(8,128)S(1)}) custom-call(s32[4]{0:T(128)S(1)} %pad_add_fusion.place_ref, bf16[8,2,192,1024]{3,2,1,0:T(8,128)(2,1)S(1)} %get-tuple-element.14.kept_ref, s32[3072,128]{1,0:T(8,128)} %cost_ref.1, f32[392,128]{1,0:T(8,128)S(1)} %fusion.4.after_ref), custom_call_target="tpu_custom_call" | custom-call | flops 3221225472 | bytes 8053063 | tf_op jit(solution)/shard_map/flip/pallas_call | solution.py:185
  23.9 1.8 %collective-permute-start.7 = (bf16[416,128]{1,0:T(8,128)(2,1)S(1)}, bf16[416,128]{1,0:T(8,128)(2,1)S(1)}, u32[]{:S(2)}, u32[]{:S(2)}) collective-permute-start(bf16[416,128]{1,0:T(8,128)(2,1)S(1)} %constant_dynamic-update-slice_fusion.16), channel_id=1, source_target_pairs={{0,48},{4,52},{8,56},{12,60},{16,0},{20,4},{24,8},{28,12},{32,16},... | collective-permute-start | bytes 319496 | tf_op jit(solution)/shard_map/gather/ppermute | solution.py:396
  25.7 0.9 collective-permute-start.6
  27.3 6.0 %collective-permute-done.5 = bf16[416,128]{1,0:T(8,128)(2,1)S(1)} collective-permute-done((bf16[416,128]{1,0:T(8,128)(2,1)S(1)}, bf16[416,128]{1,0:T(8,128)(2,1)S(1)}, u32[]{:S(2)}, u32[]{:S(2)}) %collective-permute-start.5) | collective-permute-done | bytes 106528 | tf_op jit(solution)/shard_map/gather/ppermute | solution.py:396
  33.6 1.1 loads.4
  36.3 1.6 %collective-permute-start.10 = (f32[8,128]{1,0:T(8,128)S(1)}, f32[8,128]{1,0:T(8,128)S(1)}, u32[]{:S(2)}, u32[]{:S(2)}) collective-permute-start(f32[8,128]{1,0:T(8,128)S(1)} %total.2), channel_id=1, source_target_pairs={{0,64},{64,128},{128,192},{192,0},{1,65},{65,129},{129,193},{193,1... | collective-permute-start | bytes 12296 | tf_op jit(solution)/shard_map/total/ppermute | solution.py:358
  37.9 3.5 %collective-permute-start.9 = (f32[8,128]{1,0:T(8,128)S(1)}, f32[8,128]{1,0:T(8,128)S(1)}, u32[]{:S(2)}, u32[]{:S(2)}) collective-permute-start(f32[8,128]{1,0:T(8,128)S(1)} %total.2), channel_id=1, source_target_pairs={{0,128},{64,192},{128,0},{192,64},{1,129},{65,193},{129,1},{193,65... | collective-permute-start | bytes 12296 | tf_op jit(solution)/shard_map/total/ppermute | solution.py:358
  41.4 1.1 loads.5
  43.3 1.5 %collective-permute-start.14 = (f16[1040,128]{1,0:T(8,128)(2,1)S(1)}, f16[1040,128]{1,0:T(8,128)(2,1)S(1)}, u32[]{:S(2)}, u32[]{:S(2)}) collective-permute-start(f16[1040,128]{1,0:T(8,128)(2,1)S(1)} %get-tuple-element.63), channel_id=1, source_target_pairs={{0,192},{64,0},{128,64},{192,128},{1,193},{65,1},{129,65},{193,129... | collective-permute-start | bytes 798728 | tf_op jit(solution)/shard_map/sum_y/ppermute | solution.py:411
  44.8 2.2 %collective-permute-start.13 = (f16[1040,128]{1,0:T(8,128)(2,1)S(1)}, f16[1040,128]{1,0:T(8,128)(2,1)S(1)}, u32[]{:S(2)}, u32[]{:S(2)}) collective-permute-start(f16[1040,128]{1,0:T(8,128)(2,1)S(1)} %get-tuple-element.63), channel_id=1, source_target_pairs={{0,128},{64,192},{128,0},{192,64},{1,129},{65,193},{129,1},{193,65... | collective-permute-start | bytes 798728 | tf_op jit(solution)/shard_map/sum_y/ppermute | solution.py:411
  47.0 2.5 %collective-permute-start.12 = (f16[1040,128]{1,0:T(8,128)(2,1)S(1)}, f16[1040,128]{1,0:T(8,128)(2,1)S(1)}, u32[]{:S(2)}, u32[]{:S(2)}) collective-permute-start(f16[1040,128]{1,0:T(8,128)(2,1)S(1)} %get-tuple-element.63), channel_id=1, source_target_pairs={{0,64},{64,128},{128,192},{192,0},{1,65},{65,129},{129,193},{193,1... | collective-permute-start | bytes 798728 | tf_op jit(solution)/shard_map/sum_y/ppermute | solution.py:411
  49.5 3.3 %collective-permute-start.16 = (f32[8,128]{1,0:T(8,128)S(1)}, f32[8,128]{1,0:T(8,128)S(1)}, u32[]{:S(2)}, u32[]{:S(2)}) collective-permute-start(f32[8,128]{1,0:T(8,128)S(1)} %get-tuple-element.44), channel_id=1, source_target_pairs={{0,1},{1,2},{2,3},{3,0},{4,5},{5,6},{6,7},{7,4},{8,9},{9,10},{10,1... | collective-permute-start | bytes 12296 | tf_op jit(solution)/shard_map/total/ppermute | solution.py:358
  52.8 5.0 %collective-permute-start.15 = (f32[8,128]{1,0:T(8,128)S(1)}, f32[8,128]{1,0:T(8,128)S(1)}, u32[]{:S(2)}, u32[]{:S(2)}) collective-permute-start(f32[8,128]{1,0:T(8,128)S(1)} %get-tuple-element.44), channel_id=1, source_target_pairs={{0,2},{1,3},{2,0},{3,1},{4,6},{5,7},{6,4},{7,5},{8,10},{9,11},{10,... | collective-permute-start | bytes 12296 | tf_op jit(solution)/shard_map/total/ppermute | solution.py:358
  57.7 2.7 %collective-permute-start.17 = (f32[8,128]{1,0:T(8,128)S(1)}, f32[8,128]{1,0:T(8,128)S(1)}, u32[]{:S(2)}, u32[]{:S(2)}) collective-permute-start(f32[8,128]{1,0:T(8,128)S(1)} %get-tuple-element.44), channel_id=1, source_target_pairs={{0,3},{1,0},{2,1},{3,2},{4,7},{5,4},{6,5},{7,6},{8,11},{9,8},{10,9... | collective-permute-start | bytes 12296 | tf_op jit(solution)/shard_map/total/ppermute | solution.py:358
  60.4 1.8 %collective-permute-done.17 = f32[8,128]{1,0:T(8,128)S(1)} collective-permute-done((f32[8,128]{1,0:T(8,128)S(1)}, f32[8,128]{1,0:T(8,128)S(1)}, u32[]{:S(2)}, u32[]{:S(2)}) %collective-permute-start.17) | collective-permute-done | bytes 4128 | tf_op jit(solution)/shard_map/total/ppermute | solution.py:358
  63.2 1.0 scores.7
  64.3 1.0 scores.6
  65.2 1.3 %collective-permute-done.18 = f32[1536,128]{1,0:T(8,128)S(1)} collective-permute-done((f32[1536,128]{1,0:T(8,128)S(1)}, f32[1536,128]{1,0:T(8,128)S(1)}, u32[]{:S(2)}, u32[]{:S(2)}) %collective-permute-start.18) | collective-permute-done | bytes 786464 | tf_op jit(solution)/shard_map/scores/ppermute | solution.py:380
  67.0 3.3 %collective-permute-start.21 = (s16[400,128]{1,0:T(8,128)(2,1)S(1)}, s16[400,128]{1,0:T(8,128)(2,1)S(1)}, u32[]{:S(2)}, u32[]{:S(2)}) collective-permute-start(s16[400,128]{1,0:T(8,128)(2,1)S(1)} %fusion.2), channel_id=1, source_target_pairs={{0,48},{4,52},{8,56},{12,60},{16,0},{20,4},{24,8},{28,12},{32,16},... | collective-permute-start | bytes 307208 | tf_op jit(solution)/shard_map/sum_x/ppermute | solution.py:383
  70.4 2.7 %collective-permute-done.20 = s16[400,128]{1,0:T(8,128)(2,1)S(1)} collective-permute-done((s16[400,128]{1,0:T(8,128)(2,1)S(1)}, s16[400,128]{1,0:T(8,128)(2,1)S(1)}, u32[]{:S(2)}, u32[]{:S(2)}) %collective-permute-start.20) | collective-permute-done | bytes 102432 | tf_op jit(solution)/shard_map/sum_x/ppermute | solution.py:383
  73.1 1.5 %collective-permute-done.21 = s16[400,128]{1,0:T(8,128)(2,1)S(1)} collective-permute-done((s16[400,128]{1,0:T(8,128)(2,1)S(1)}, s16[400,128]{1,0:T(8,128)(2,1)S(1)}, u32[]{:S(2)}, u32[]{:S(2)}) %collective-permute-start.21) | collective-permute-done | bytes 102432 | tf_op jit(solution)/shard_map/sum_x/ppermute | solution.py:383
  74.7 1.9 %collective-permute-done.19 = s16[400,128]{1,0:T(8,128)(2,1)S(1)} collective-permute-done((s16[400,128]{1,0:T(8,128)(2,1)S(1)}, s16[400,128]{1,0:T(8,128)(2,1)S(1)}, u32[]{:S(2)}, u32[]{:S(2)}) %collective-permute-start.19) | collective-permute-done | bytes 102432 | tf_op jit(solution)/shard_map/sum_x/ppermute | solution.py:383
  76.8 1.1 collective-permute-start.22
  77.9 3.6 %collective-permute-done.22 = s16[400,128]{1,0:T(8,128)(2,1)S(1)} collective-permute-done((s16[400,128]{1,0:T(8,128)(2,1)S(1)}, s16[400,128]{1,0:T(8,128)(2,1)S(1)}, u32[]{:S(2)}, u32[]{:S(2)}) %collective-permute-start.22) | collective-permute-done | bytes 102432 | tf_op jit(solution)/shard_map/sum_z/ppermute | solution.py:389
  81.7 2.1 %collective-permute-start.25 = (bf16[384,128]{1,0:T(8,128)(2,1)S(1)}, bf16[384,128]{1,0:T(8,128)(2,1)S(1)}, u32[]{:S(2)}, u32[]{:S(2)}) collective-permute-start(bf16[384,128]{1,0:T(8,128)(2,1)S(1)} %get-tuple-element.31), channel_id=1, source_target_pairs={{0,48},{4,52},{8,56},{12,60},{16,0},{20,4},{24,8},{28,12},{32,16},... | collective-permute-start | bytes 294920 | tf_op jit(solution)/shard_map/gather/ppermute | solution.py:396
  83.8 1.0 collective-permute-start.23
  84.8 2.3 %collective-permute-done.25 = bf16[384,128]{1,0:T(8,128)(2,1)S(1)} collective-permute-done((bf16[384,128]{1,0:T(8,128)(2,1)S(1)}, bf16[384,128]{1,0:T(8,128)(2,1)S(1)}, u32[]{:S(2)}, u32[]{:S(2)}) %collective-permute-start.25) | collective-permute-done | bytes 98336 | tf_op jit(solution)/shard_map/gather/ppermute | solution.py:396
  87.0 3.0 %collective-permute-done.24 = bf16[384,128]{1,0:T(8,128)(2,1)S(1)} collective-permute-done((bf16[384,128]{1,0:T(8,128)(2,1)S(1)}, bf16[384,128]{1,0:T(8,128)(2,1)S(1)}, u32[]{:S(2)}, u32[]{:S(2)}) %collective-permute-start.24) | collective-permute-done | bytes 98336 | tf_op jit(solution)/shard_map/gather/ppermute | solution.py:396
  90.8 1.1 loads.6
  93.1 2.0 %collective-permute-start.28 = (f32[8,128]{1,0:T(8,128)S(1)}, f32[8,128]{1,0:T(8,128)S(1)}, u32[]{:S(2)}, u32[]{:S(2)}) collective-permute-start(f32[8,128]{1,0:T(8,128)S(1)} %total.3), channel_id=1, source_target_pairs={{0,64},{64,128},{128,192},{192,0},{1,65},{65,129},{129,193},{193,1... | collective-permute-start | bytes 12296 | tf_op jit(solution)/shard_map/total/ppermute | solution.py:358
  95.1 1.8 %collective-permute-start.27 = (f32[8,128]{1,0:T(8,128)S(1)}, f32[8,128]{1,0:T(8,128)S(1)}, u32[]{:S(2)}, u32[]{:S(2)}) collective-permute-start(f32[8,128]{1,0:T(8,128)S(1)} %total.3), channel_id=1, source_target_pairs={{0,128},{64,192},{128,0},{192,64},{1,129},{65,193},{129,1},{193,65... | collective-permute-start | bytes 12296 | tf_op jit(solution)/shard_map/total/ppermute | solution.py:358
  96.9 1.1 loads.7
  98.1 2.1 %collective-permute-done.27 = f32[8,128]{1,0:T(8,128)S(1)} collective-permute-done((f32[8,128]{1,0:T(8,128)S(1)}, f32[8,128]{1,0:T(8,128)S(1)}, u32[]{:S(2)}, u32[]{:S(2)}) %collective-permute-start.27) | collective-permute-done | bytes 4128 | tf_op jit(solution)/shard_map/total/ppermute | solution.py:358
  100.7 1.8 %collective-permute-start.31 = (f16[1040,128]{1,0:T(8,128)(2,1)S(1)}, f16[1040,128]{1,0:T(8,128)(2,1)S(1)}, u32[]{:S(2)}, u32[]{:S(2)}) collective-permute-start(f16[1040,128]{1,0:T(8,128)(2,1)S(1)} %get-tuple-element.61), channel_id=1, source_target_pairs={{0,128},{64,192},{128,0},{192,64},{1,129},{65,193},{129,1},{193,65... | collective-permute-start | bytes 798728 | tf_op jit(solution)/shard_map/sum_y/ppermute | solution.py:411
  102.5 2.5 %collective-permute-start.30 = (f16[1040,128]{1,0:T(8,128)(2,1)S(1)}, f16[1040,128]{1,0:T(8,128)(2,1)S(1)}, u32[]{:S(2)}, u32[]{:S(2)}) collective-permute-start(f16[1040,128]{1,0:T(8,128)(2,1)S(1)} %get-tuple-element.61), channel_id=1, source_target_pairs={{0,64},{64,128},{128,192},{192,0},{1,65},{65,129},{129,193},{193,1... | collective-permute-start | bytes 798728 | tf_op jit(solution)/shard_map/sum_y/ppermute | solution.py:411
  105.0 2.1 %collective-permute-start.34 = (f32[8,128]{1,0:T(8,128)S(1)}, f32[8,128]{1,0:T(8,128)S(1)}, u32[]{:S(2)}, u32[]{:S(2)}) collective-permute-start(f32[8,128]{1,0:T(8,128)S(1)} %get-tuple-element.30), channel_id=1, source_target_pairs={{0,1},{1,2},{2,3},{3,0},{4,5},{5,6},{6,7},{7,4},{8,9},{9,10},{10,1... | collective-permute-start | bytes 12296 | tf_op jit(solution)/shard_map/total/ppermute | solution.py:358
  107.1 4.3 %collective-permute-start.33 = (f32[8,128]{1,0:T(8,128)S(1)}, f32[8,128]{1,0:T(8,128)S(1)}, u32[]{:S(2)}, u32[]{:S(2)}) collective-permute-start(f32[8,128]{1,0:T(8,128)S(1)} %get-tuple-element.30), channel_id=1, source_target_pairs={{0,2},{1,3},{2,0},{3,1},{4,6},{5,7},{6,4},{7,5},{8,10},{9,11},{10,... | collective-permute-start | bytes 12296 | tf_op jit(solution)/shard_map/total/ppermute | solution.py:358
  111.4 2.7 %collective-permute-start.35 = (f32[8,128]{1,0:T(8,128)S(1)}, f32[8,128]{1,0:T(8,128)S(1)}, u32[]{:S(2)}, u32[]{:S(2)}) collective-permute-start(f32[8,128]{1,0:T(8,128)S(1)} %get-tuple-element.30), channel_id=1, source_target_pairs={{0,3},{1,0},{2,1},{3,2},{4,7},{5,4},{6,5},{7,6},{8,11},{9,8},{10,9... | collective-permute-start | bytes 12296 | tf_op jit(solution)/shard_map/total/ppermute | solution.py:358
  114.7 1.2 %collective-permute-done.35 = f32[8,128]{1,0:T(8,128)S(1)} collective-permute-done((f32[8,128]{1,0:T(8,128)S(1)}, f32[8,128]{1,0:T(8,128)S(1)}, u32[]{:S(2)}, u32[]{:S(2)}) %collective-permute-start.35) | collective-permute-done | bytes 4128 | tf_op jit(solution)/shard_map/total/ppermute | solution.py:358
  116.1 1.6 %update.3 = (f32[1024,128]{1,0:T(8,128)}, f32[192,128]{1,0:T(8,128)}) custom-call(s32[4]{0:T(128)S(1)} %pad_add_fusion.place_ref, f32[1040,128]{1,0:T(8,128)S(1)} %get-tuple-element.62.zero, f32[1040,128]{1,0:T(8,128)S(1)} %convert_element_type.134.one, f32[1040,128]{1,0:T(8,128)S(1)} %convert_element_type.135.two, ...), custom_call_target="tpu_custom_call" | custom-call | flops 10000000 | bytes 25000 | tf_op jit(solution)/shard_map/update/pallas_call | solution.py:340
  (115 shorter events, 9.7 us)
Async XLA Ops:
  5.8 2.4 %collective-permute-start = (f32[1568,128]{1,0:T(8,128)S(1)}, f32[1568,128]{1,0:T(8,128)S(1)}, u32[]{:S(2)}, u32[]{:S(2)}) collective-permute-start(f32[1568,128]{1,0:T(8,128)S(1)} %get-tuple-element.16), channel_id=1, source_target_pairs={{0,4},{4,0},{8,12},{12,8},{16,20},{20,16},{24,28},{28,24},{32,36},... | collective-permute-start | bytes 2408456 | tf_op jit(solution)/shard_map/scores/ppermute | solution.py:380
  8.4 10.2 %collective-permute-start.1 = (bf16[416,128]{1,0:T(8,128)(2,1)S(1)}, bf16[416,128]{1,0:T(8,128)(2,1)S(1)}, u32[]{:S(2)}, u32[]{:S(2)}) collective-permute-start(bf16[416,128]{1,0:T(8,128)(2,1)S(1)} %constant_dynamic-update-slice_fusion), channel_id=1, source_target_pairs={{0,32},{4,36},{8,40},{12,44},{16,48},{20,52},{24,56},{28,60},{32,0... | collective-permute-start | bytes 319496 | tf_op jit(solution)/shard_map/sum_x/ppermute | solution.py:383
  11.6 5.9 %collective-permute-start.3 = (bf16[416,128]{1,0:T(8,128)(2,1)S(1)}, bf16[416,128]{1,0:T(8,128)(2,1)S(1)}, u32[]{:S(2)}, u32[]{:S(2)}) collective-permute-start(bf16[416,128]{1,0:T(8,128)(2,1)S(1)} %constant_dynamic-update-slice_fusion.8), channel_id=1, source_target_pairs={{0,48},{4,52},{8,56},{12,60},{16,0},{20,4},{24,8},{28,12},{32,16},... | collective-permute-start | bytes 319496 | tf_op jit(solution)/shard_map/sum_x/ppermute | solution.py:383
  12.7 5.9 %collective-permute-start.2 = (bf16[416,128]{1,0:T(8,128)(2,1)S(1)}, bf16[416,128]{1,0:T(8,128)(2,1)S(1)}, u32[]{:S(2)}, u32[]{:S(2)}) collective-permute-start(bf16[416,128]{1,0:T(8,128)(2,1)S(1)} %constant_dynamic-update-slice_fusion.4), channel_id=1, source_target_pairs={{0,16},{4,20},{8,24},{12,28},{16,32},{20,36},{24,40},{28,44},{32,4... | collective-permute-start | bytes 319496 | tf_op jit(solution)/shard_map/sum_x/ppermute | solution.py:383
  18.9 4.8 %collective-permute-start.4 = (bf16[416,128]{1,0:T(8,128)(2,1)S(1)}, bf16[416,128]{1,0:T(8,128)(2,1)S(1)}, u32[]{:S(2)}, u32[]{:S(2)}) collective-permute-start(bf16[416,128]{1,0:T(8,128)(2,1)S(1)} %constant_dynamic-update-slice_fusion.12), channel_id=1, source_target_pairs={{0,8},{4,12},{8,0},{12,4},{16,24},{20,28},{24,16},{28,20},{32,40},... | collective-permute-start | bytes 319496 | tf_op jit(solution)/shard_map/sum_z/ppermute | solution.py:389
  23.9 9.5 %collective-permute-start.7 = (bf16[416,128]{1,0:T(8,128)(2,1)S(1)}, bf16[416,128]{1,0:T(8,128)(2,1)S(1)}, u32[]{:S(2)}, u32[]{:S(2)}) collective-permute-start(bf16[416,128]{1,0:T(8,128)(2,1)S(1)} %constant_dynamic-update-slice_fusion.16), channel_id=1, source_target_pairs={{0,48},{4,52},{8,56},{12,60},{16,0},{20,4},{24,8},{28,12},{32,16},... | collective-permute-start | bytes 319496 | tf_op jit(solution)/shard_map/gather/ppermute | solution.py:396
  25.7 7.7 %collective-permute-start.6 = (bf16[416,128]{1,0:T(8,128)(2,1)S(1)}, bf16[416,128]{1,0:T(8,128)(2,1)S(1)}, u32[]{:S(2)}, u32[]{:S(2)}) collective-permute-start(bf16[416,128]{1,0:T(8,128)(2,1)S(1)} %constant_dynamic-update-slice_fusion.16), channel_id=1, source_target_pairs={{0,32},{4,36},{8,40},{12,44},{16,48},{20,52},{24,56},{28,60},{32,0... | collective-permute-start | bytes 319496 | tf_op jit(solution)/shard_map/gather/ppermute | solution.py:396
  26.7 6.7 %collective-permute-start.5 = (bf16[416,128]{1,0:T(8,128)(2,1)S(1)}, bf16[416,128]{1,0:T(8,128)(2,1)S(1)}, u32[]{:S(2)}, u32[]{:S(2)}) collective-permute-start(bf16[416,128]{1,0:T(8,128)(2,1)S(1)} %constant_dynamic-update-slice_fusion.16), channel_id=1, source_target_pairs={{0,16},{4,20},{8,24},{12,28},{16,32},{20,36},{24,40},{28,44},{32,4... | collective-permute-start | bytes 319496 | tf_op jit(solution)/shard_map/gather/ppermute | solution.py:396
  33.5 1.9 %collective-permute-start.8 = (bf16[1664,128]{1,0:T(8,128)(2,1)S(1)}, bf16[1664,128]{1,0:T(8,128)(2,1)S(1)}, u32[]{:S(2)}, u32[]{:S(2)}) collective-permute-start(bf16[1664,128]{1,0:T(8,128)(2,1)S(1)} %constant_dynamic-update-slice_fusion.21.low_ref.sums_own.low_own), channel_id=1, source_target_pairs={{0,4},{4,0},{8,12},{12,8},{16,20},{20,16},{24,28},{28,24},{32,36},... | collective-permute-start | bytes 1277960 | tf_op jit(solution)/shard_map/gather/ppermute | solution.py:398
  35.8 6.8 %collective-permute-start.11 = (f32[8,128]{1,0:T(8,128)S(1)}, f32[8,128]{1,0:T(8,128)S(1)}, u32[]{:S(2)}, u32[]{:S(2)}) collective-permute-start(f32[8,128]{1,0:T(8,128)S(1)} %total.2), channel_id=1, source_target_pairs={{0,192},{64,0},{128,64},{192,128},{1,193},{65,1},{129,65},{193,129... | collective-permute-start | bytes 12296 | tf_op jit(solution)/shard_map/total/ppermute | solution.py:358
  36.3 6.3 %collective-permute-start.10 = (f32[8,128]{1,0:T(8,128)S(1)}, f32[8,128]{1,0:T(8,128)S(1)}, u32[]{:S(2)}, u32[]{:S(2)}) collective-permute-start(f32[8,128]{1,0:T(8,128)S(1)} %total.2), channel_id=1, source_target_pairs={{0,64},{64,128},{128,192},{192,0},{1,65},{65,129},{129,193},{193,1... | collective-permute-start | bytes 12296 | tf_op jit(solution)/shard_map/total/ppermute | solution.py:358
  37.9 5.1 %collective-permute-start.9 = (f32[8,128]{1,0:T(8,128)S(1)}, f32[8,128]{1,0:T(8,128)S(1)}, u32[]{:S(2)}, u32[]{:S(2)}) collective-permute-start(f32[8,128]{1,0:T(8,128)S(1)} %total.2), channel_id=1, source_target_pairs={{0,128},{64,192},{128,0},{192,64},{1,129},{65,193},{129,1},{193,65... | collective-permute-start | bytes 12296 | tf_op jit(solution)/shard_map/total/ppermute | solution.py:358
  43.3 19.0 %collective-permute-start.14 = (f16[1040,128]{1,0:T(8,128)(2,1)S(1)}, f16[1040,128]{1,0:T(8,128)(2,1)S(1)}, u32[]{:S(2)}, u32[]{:S(2)}) collective-permute-start(f16[1040,128]{1,0:T(8,128)(2,1)S(1)} %get-tuple-element.63), channel_id=1, source_target_pairs={{0,192},{64,0},{128,64},{192,128},{1,193},{65,1},{129,65},{193,129... | collective-permute-start | bytes 798728 | tf_op jit(solution)/shard_map/sum_y/ppermute | solution.py:411
  44.8 17.5 %collective-permute-start.13 = (f16[1040,128]{1,0:T(8,128)(2,1)S(1)}, f16[1040,128]{1,0:T(8,128)(2,1)S(1)}, u32[]{:S(2)}, u32[]{:S(2)}) collective-permute-start(f16[1040,128]{1,0:T(8,128)(2,1)S(1)} %get-tuple-element.63), channel_id=1, source_target_pairs={{0,128},{64,192},{128,0},{192,64},{1,129},{65,193},{129,1},{193,65... | collective-permute-start | bytes 798728 | tf_op jit(solution)/shard_map/sum_y/ppermute | solution.py:411
  47.0 15.4 %collective-permute-start.12 = (f16[1040,128]{1,0:T(8,128)(2,1)S(1)}, f16[1040,128]{1,0:T(8,128)(2,1)S(1)}, u32[]{:S(2)}, u32[]{:S(2)}) collective-permute-start(f16[1040,128]{1,0:T(8,128)(2,1)S(1)} %get-tuple-element.63), channel_id=1, source_target_pairs={{0,64},{64,128},{128,192},{192,0},{1,65},{65,129},{129,193},{193,1... | collective-permute-start | bytes 798728 | tf_op jit(solution)/shard_map/sum_y/ppermute | solution.py:411
  49.5 8.2 %collective-permute-start.16 = (f32[8,128]{1,0:T(8,128)S(1)}, f32[8,128]{1,0:T(8,128)S(1)}, u32[]{:S(2)}, u32[]{:S(2)}) collective-permute-start(f32[8,128]{1,0:T(8,128)S(1)} %get-tuple-element.44), channel_id=1, source_target_pairs={{0,1},{1,2},{2,3},{3,0},{4,5},{5,6},{6,7},{7,4},{8,9},{9,10},{10,1... | collective-permute-start | bytes 12296 | tf_op jit(solution)/shard_map/total/ppermute | solution.py:358
  52.8 7.6 %collective-permute-start.15 = (f32[8,128]{1,0:T(8,128)S(1)}, f32[8,128]{1,0:T(8,128)S(1)}, u32[]{:S(2)}, u32[]{:S(2)}) collective-permute-start(f32[8,128]{1,0:T(8,128)S(1)} %get-tuple-element.44), channel_id=1, source_target_pairs={{0,2},{1,3},{2,0},{3,1},{4,6},{5,7},{6,4},{7,5},{8,10},{9,11},{10,... | collective-permute-start | bytes 12296 | tf_op jit(solution)/shard_map/total/ppermute | solution.py:358
  57.7 4.5 %collective-permute-start.17 = (f32[8,128]{1,0:T(8,128)S(1)}, f32[8,128]{1,0:T(8,128)S(1)}, u32[]{:S(2)}, u32[]{:S(2)}) collective-permute-start(f32[8,128]{1,0:T(8,128)S(1)} %get-tuple-element.44), channel_id=1, source_target_pairs={{0,3},{1,0},{2,1},{3,2},{4,7},{5,4},{6,5},{7,6},{8,11},{9,8},{10,9... | collective-permute-start | bytes 12296 | tf_op jit(solution)/shard_map/total/ppermute | solution.py:358
  64.2 2.4 %collective-permute-start.18 = (f32[1536,128]{1,0:T(8,128)S(1)}, f32[1536,128]{1,0:T(8,128)S(1)}, u32[]{:S(2)}, u32[]{:S(2)}) collective-permute-start(f32[1536,128]{1,0:T(8,128)S(1)} %scores.7), channel_id=1, source_target_pairs={{0,4},{4,0},{8,12},{12,8},{16,20},{20,16},{24,28},{28,24},{32,36},... | collective-permute-start | bytes 2359304 | tf_op jit(solution)/shard_map/scores/ppermute | solution.py:380
  66.9 6.2 %collective-permute-start.20 = (s16[400,128]{1,0:T(8,128)(2,1)S(1)}, s16[400,128]{1,0:T(8,128)(2,1)S(1)}, u32[]{:S(2)}, u32[]{:S(2)}) collective-permute-start(s16[400,128]{1,0:T(8,128)(2,1)S(1)} %fusion.1), channel_id=1, source_target_pairs={{0,16},{4,20},{8,24},{12,28},{16,32},{20,36},{24,40},{28,44},{32,4... | collective-permute-start | bytes 307208 | tf_op jit(solution)/shard_map/sum_x/ppermute | solution.py:383
  67.0 7.6 %collective-permute-start.21 = (s16[400,128]{1,0:T(8,128)(2,1)S(1)}, s16[400,128]{1,0:T(8,128)(2,1)S(1)}, u32[]{:S(2)}, u32[]{:S(2)}) collective-permute-start(s16[400,128]{1,0:T(8,128)(2,1)S(1)} %fusion.2), channel_id=1, source_target_pairs={{0,48},{4,52},{8,56},{12,60},{16,0},{20,4},{24,8},{28,12},{32,16},... | collective-permute-start | bytes 307208 | tf_op jit(solution)/shard_map/sum_x/ppermute | solution.py:383
  70.3 6.3 %collective-permute-start.19 = (s16[400,128]{1,0:T(8,128)(2,1)S(1)}, s16[400,128]{1,0:T(8,128)(2,1)S(1)}, u32[]{:S(2)}, u32[]{:S(2)}) collective-permute-start(s16[400,128]{1,0:T(8,128)(2,1)S(1)} %fusion), channel_id=1, source_target_pairs={{0,32},{4,36},{8,40},{12,44},{16,48},{20,52},{24,56},{28,60},{32,0... | collective-permute-start | bytes 307208 | tf_op jit(solution)/shard_map/sum_x/ppermute | solution.py:383
  76.8 4.7 %collective-permute-start.22 = (s16[400,128]{1,0:T(8,128)(2,1)S(1)}, s16[400,128]{1,0:T(8,128)(2,1)S(1)}, u32[]{:S(2)}, u32[]{:S(2)}) collective-permute-start(s16[400,128]{1,0:T(8,128)(2,1)S(1)} %fusion.3), channel_id=1, source_target_pairs={{0,8},{4,12},{8,0},{12,4},{16,24},{20,28},{24,16},{28,20},{32,40},... | collective-permute-start | bytes 307208 | tf_op jit(solution)/shard_map/sum_z/ppermute | solution.py:389
  81.7 5.4 %collective-permute-start.25 = (bf16[384,128]{1,0:T(8,128)(2,1)S(1)}, bf16[384,128]{1,0:T(8,128)(2,1)S(1)}, u32[]{:S(2)}, u32[]{:S(2)}) collective-permute-start(bf16[384,128]{1,0:T(8,128)(2,1)S(1)} %get-tuple-element.31), channel_id=1, source_target_pairs={{0,48},{4,52},{8,56},{12,60},{16,0},{20,4},{24,8},{28,12},{32,16},... | collective-permute-start | bytes 294920 | tf_op jit(solution)/shard_map/gather/ppermute | solution.py:396
  83.8 6.2 %collective-permute-start.24 = (bf16[384,128]{1,0:T(8,128)(2,1)S(1)}, bf16[384,128]{1,0:T(8,128)(2,1)S(1)}, u32[]{:S(2)}, u32[]{:S(2)}) collective-permute-start(bf16[384,128]{1,0:T(8,128)(2,1)S(1)} %get-tuple-element.31), channel_id=1, source_target_pairs={{0,32},{4,36},{8,40},{12,44},{16,48},{20,52},{24,56},{28,60},{32,0... | collective-permute-start | bytes 294920 | tf_op jit(solution)/shard_map/gather/ppermute | solution.py:396
  83.8 6.9 %collective-permute-start.23 = (bf16[384,128]{1,0:T(8,128)(2,1)S(1)}, bf16[384,128]{1,0:T(8,128)(2,1)S(1)}, u32[]{:S(2)}, u32[]{:S(2)}) collective-permute-start(bf16[384,128]{1,0:T(8,128)(2,1)S(1)} %get-tuple-element.31), channel_id=1, source_target_pairs={{0,16},{4,20},{8,24},{12,28},{16,32},{20,36},{24,40},{28,44},{32,4... | collective-permute-start | bytes 294920 | tf_op jit(solution)/shard_map/gather/ppermute | solution.py:396
  90.7 1.8 %collective-permute-start.26 = (bf16[1536,128]{1,0:T(8,128)(2,1)S(1)}, bf16[1536,128]{1,0:T(8,128)(2,1)S(1)}, u32[]{:S(2)}, u32[]{:S(2)}) collective-permute-start(bf16[1536,128]{1,0:T(8,128)(2,1)S(1)} %pad_maximum_fusion.low_ref.low_own), channel_id=1, source_target_pairs={{0,4},{4,0},{8,12},{12,8},{16,20},{20,16},{24,28},{28,24},{32,36},... | collective-permute-start | bytes 1179656 | tf_op jit(solution)/shard_map/gather/ppermute | solution.py:398
  93.0 5.1 %collective-permute-start.29 = (f32[8,128]{1,0:T(8,128)S(1)}, f32[8,128]{1,0:T(8,128)S(1)}, u32[]{:S(2)}, u32[]{:S(2)}) collective-permute-start(f32[8,128]{1,0:T(8,128)S(1)} %total.3), channel_id=1, source_target_pairs={{0,192},{64,0},{128,64},{192,128},{1,193},{65,1},{129,65},{193,129... | collective-permute-start | bytes 12296 | tf_op jit(solution)/shard_map/total/ppermute | solution.py:358
  93.1 5.0 %collective-permute-start.28 = (f32[8,128]{1,0:T(8,128)S(1)}, f32[8,128]{1,0:T(8,128)S(1)}, u32[]{:S(2)}, u32[]{:S(2)}) collective-permute-start(f32[8,128]{1,0:T(8,128)S(1)} %total.3), channel_id=1, source_target_pairs={{0,64},{64,128},{128,192},{192,0},{1,65},{65,129},{129,193},{193,1... | collective-permute-start | bytes 12296 | tf_op jit(solution)/shard_map/total/ppermute | solution.py:358
  95.1 5.1 %collective-permute-start.27 = (f32[8,128]{1,0:T(8,128)S(1)}, f32[8,128]{1,0:T(8,128)S(1)}, u32[]{:S(2)}, u32[]{:S(2)}) collective-permute-start(f32[8,128]{1,0:T(8,128)S(1)} %total.3), channel_id=1, source_target_pairs={{0,128},{64,192},{128,0},{192,64},{1,129},{65,193},{129,1},{193,65... | collective-permute-start | bytes 12296 | tf_op jit(solution)/shard_map/total/ppermute | solution.py:358
  100.5 15.4 %collective-permute-start.32 = (f16[1040,128]{1,0:T(8,128)(2,1)S(1)}, f16[1040,128]{1,0:T(8,128)(2,1)S(1)}, u32[]{:S(2)}, u32[]{:S(2)}) collective-permute-start(f16[1040,128]{1,0:T(8,128)(2,1)S(1)} %get-tuple-element.61), channel_id=1, source_target_pairs={{0,192},{64,0},{128,64},{192,128},{1,193},{65,1},{129,65},{193,129... | collective-permute-start | bytes 798728 | tf_op jit(solution)/shard_map/sum_y/ppermute | solution.py:411
  100.7 15.3 %collective-permute-start.31 = (f16[1040,128]{1,0:T(8,128)(2,1)S(1)}, f16[1040,128]{1,0:T(8,128)(2,1)S(1)}, u32[]{:S(2)}, u32[]{:S(2)}) collective-permute-start(f16[1040,128]{1,0:T(8,128)(2,1)S(1)} %get-tuple-element.61), channel_id=1, source_target_pairs={{0,128},{64,192},{128,0},{192,64},{1,129},{65,193},{129,1},{193,65... | collective-permute-start | bytes 798728 | tf_op jit(solution)/shard_map/sum_y/ppermute | solution.py:411
  102.5 13.5 %collective-permute-start.30 = (f16[1040,128]{1,0:T(8,128)(2,1)S(1)}, f16[1040,128]{1,0:T(8,128)(2,1)S(1)}, u32[]{:S(2)}, u32[]{:S(2)}) collective-permute-start(f16[1040,128]{1,0:T(8,128)(2,1)S(1)} %get-tuple-element.61), channel_id=1, source_target_pairs={{0,64},{64,128},{128,192},{192,0},{1,65},{65,129},{129,193},{193,1... | collective-permute-start | bytes 798728 | tf_op jit(solution)/shard_map/sum_y/ppermute | solution.py:411
  105.0 6.4 %collective-permute-start.34 = (f32[8,128]{1,0:T(8,128)S(1)}, f32[8,128]{1,0:T(8,128)S(1)}, u32[]{:S(2)}, u32[]{:S(2)}) collective-permute-start(f32[8,128]{1,0:T(8,128)S(1)} %get-tuple-element.30), channel_id=1, source_target_pairs={{0,1},{1,2},{2,3},{3,0},{4,5},{5,6},{6,7},{7,4},{8,9},{9,10},{10,1... | collective-permute-start | bytes 12296 | tf_op jit(solution)/shard_map/total/ppermute | solution.py:358
  107.1 7.6 %collective-permute-start.33 = (f32[8,128]{1,0:T(8,128)S(1)}, f32[8,128]{1,0:T(8,128)S(1)}, u32[]{:S(2)}, u32[]{:S(2)}) collective-permute-start(f32[8,128]{1,0:T(8,128)S(1)} %get-tuple-element.30), channel_id=1, source_target_pairs={{0,2},{1,3},{2,0},{3,1},{4,6},{5,7},{6,4},{7,5},{8,10},{9,11},{10,... | collective-permute-start | bytes 12296 | tf_op jit(solution)/shard_map/total/ppermute | solution.py:358
  111.4 4.5 %collective-permute-start.35 = (f32[8,128]{1,0:T(8,128)S(1)}, f32[8,128]{1,0:T(8,128)S(1)}, u32[]{:S(2)}, u32[]{:S(2)}) collective-permute-start(f32[8,128]{1,0:T(8,128)S(1)} %get-tuple-element.30), channel_id=1, source_target_pairs={{0,3},{1,0},{2,1},{3,2},{4,7},{5,4},{6,5},{7,6},{8,11},{9,8},{10,9... | collective-permute-start | bytes 12296 | tf_op jit(solution)/shard_map/total/ppermute | solution.py:358

commit v2 on v1

--- a/solution.py
+++ b/solution.py
@@ -52,11 +52,11 @@
 
 
 def scores_and_sums(kept, weights, out_ref, d):
-    at = d * WITH_SUMS
-    out_ref[at : at + PAIR, :] = jnp.dot(kept, weights, preferred_element_type=f32)
+    at = pl.multiple_of(d * WITH_SUMS, 8)
+    out_ref[pl.ds(at, PAIR), :] = jnp.dot(kept, weights, preferred_element_type=f32)
     ones = jnp.ones((8, kept.shape[1]), bf16)
     sums = lax.dot_general(ones, kept, (((1,), (1,)), ((), ())), preferred_element_type=f32)
-    out_ref[at + PAIR : at + WITH_SUMS, :] = jnp.concatenate(
+    out_ref[pl.ds(at + PAIR, 8), :] = jnp.concatenate(
         [sums[:1, j * BLOCK : (j + 1) * BLOCK] for j in range(3)] + [jnp.zeros((5, BLOCK), f32)], axis=0
     )
 
@@ -108,8 +108,11 @@
 
 
 def own_scores_kernel(kept_ref, weights_ref, out_ref):
-    for d in range(4):
+    def step(d, carry):
         scores_and_sums(tests_of(kept_ref, d, 0), weights_ref[...], out_ref, d)
+        return carry
+
+    lax.fori_loop(0, 4, step, 0)
 
 
 def first_scores(cover, mask, prior, place):
@@ -245,15 +248,14 @@
     )(in_vmem(flipped), low, load, size)
 
 
-def total_kernel(sums_own, sums_away, low_own, low_away, out_ref):
+def total_kernel(sums_ref, low_ref, out_ref):
     totals = [jnp.zeros((32, BLOCK), f32) for _ in range(3)]
-    stride = low_own.shape[0] // 4
-    for sums_ref, low_ref in ((sums_own, low_own), (sums_away, low_away)):
-        for d in range(4):
-            sums = sums_ref[d * GATHERED + PAIR : (d + 1) * GATHERED, :]
-            for j in range(3):
-                low = low_ref[d * stride + j * BLOCK : d * stride + (j + 1) * BLOCK, :]
-                totals[j] += jnp.dot(sums, low, preferred_element_type=f32)
+    stride = low_ref.shape[0] // 4
+    for d in range(4):
+        sums = sums_ref[d * GATHERED + PAIR : (d + 1) * GATHERED, :]
+        for j in range(3):
+            low = low_ref[d * stride + j * BLOCK : d * stride + (j + 1) * BLOCK, :]
+            totals[j] += jnp.dot(sums, low, preferred_element_type=f32)
     row = lax.broadcasted_iota(jnp.int32, (32, BLOCK), 0)
     total = jnp.zeros((32, BLOCK), f32)
     for j in range(3):
@@ -261,14 +263,14 @@
     out_ref[...] = jnp.full(out_ref.shape, jnp.sum(total), f32)
 
 
-def total_load(sums_own, sums_away, low_own, low_away):
+def total_load(sums, low):
     return call(
         total_kernel,
-        jax.ShapeDtypeStruct((8, low_own.shape[1]), f32),
-        [IN_VMEM] * 4,
+        jax.ShapeDtypeStruct((8, low.shape[1]), f32),
+        [IN_VMEM] * 2,
         IN_VMEM,
         10**8,
-    )(sums_own, sums_away, low_own, low_away)
+    )(sums, low)
 
 
 def bf16_parts(sums):
@@ -320,14 +322,18 @@
         out_ref, low_ref = rest
     wires = (zero, one, two, three)
     factors = [-0.25 * jnp.exp2(wire[edges : edges + 1, :] - 11.0) / mean for wire in wires]
-    part = 128
-    for n in range(edges // part):
-        rows = slice(n * part, (n + 1) * part)
+    part = 256
+
+    def step(n, carry):
+        rows = pl.ds(pl.multiple_of(n * part, part), part)
         loads = [wire[rows, :] * factor for wire, factor in zip(wires, factors, strict=True)]
         new = current_ref[rows, :].astype(f32) * jnp.exp((loads[0] + loads[2]) + (loads[1] + loads[3]))
         out_ref[rows, :] = new
         if not last:
             low_ref[rows, :] = new.astype(bf16)
+        return carry
+
+    lax.fori_loop(0, edges // part, step, 0)
 
 
 def update(wires, total, current, place, ratios=None):
@@ -397,10 +403,11 @@
             low_here = jnp.concatenate(lows, axis=0)
             low_away = lax.ppermute(low_here, "col", swap(1))
             if first:
-                sums_here, sums_away = low_here, low_away
+                sums_here = low_here
         with jax.named_scope("total"):
-            total = total_load(sums_here, sums_away, low_here, low_away)
+            total = total_load(sums_here, low_here)
             total = row_total = sum_ring(total, "row")
+            total = total + lax.ppermute(total, "col", swap(1))
             total = sum_ring(total, "depth")
         with jax.named_scope("loads"):
             load, size = half_loads(flipped_here, low_here)

time: 119 us -> 124 us (1.042)
  waiting for transfers between devices: 36.2 us -> 44.2 us
  starting transfers between devices: 58.8 us -> 56.5 us
    ppermute x12, waiting for transfers between devices: 6.2 us -> 13.5 us  [sum_ring(): lax.ppermute(value, axis, ring(4, d))]
    ppermute x12, starting transfers between devices: 29.5 us -> 26.8 us  [sum_ring(): lax.ppermute(value, axis, ring(4, d))]
    ppermute x0 -> x2, waiting for transfers between devices: none -> 2.33 us  [body(): total = total + lax.ppermute(total, 'col', swap(1))]
    ppermute x2, waiting for transfers between devices: 1.33 us -> 0.01 us  [body(): low_away = lax.ppermute(low_here, 'col', swap(1))]
  transfers between devices with their start and end apart: 36 -> 38, of which waited for: 20 -> 23; matrix products, arithmetic and copies ran while one was open for 0% -> 0% of each run, Pallas kernels for 8% -> 7%
where the time goes in v2:
time: 124 us
  starting transfers between devices  56.5 us (46%)
  waiting for transfers between devices  44.2 us (36%)
  Pallas kernels  19.3 us (16%)
  other arithmetic  2.08 us (2%)
  between operations  1.32 us (1%)
    ppermute x12, starting transfers between devices, sum_ring(): lax.ppermute(value, axis, ring(4, d))  26.8 us
    ppermute x12, waiting for transfers between devices, sum_ring(): lax.ppermute(value, axis, ring(4, d))  13.5 us
    ppermute x6, waiting for transfers between devices, body(): lax.ppermute(low_ratios, 'col', ring(16, d, 4))  12.1 us
    ppermute x6, waiting for transfers between devices, body(): lax.ppermute(pack(here[d]), 'col', ring(16, d, 4))  11.1 us
    ppermute x6, starting transfers between devices, body(): lax.ppermute(sent, 'row', ring(4, d)).astype(f32)  10.7 us
    ppermute x6, starting transfers between devices, body(): lax.ppermute(pack(here[d]), 'col', ring(16, d, 4))  8.6 us
    ppermute x6, starting transfers between devices, body(): lax.ppermute(low_ratios, 'col', ring(16, d, 4))  6.71 us
    pallas_call x1, Pallas kernels, first_scores(): call(first_scores_kernel, [pltpu.VMEM((4 * WITH_SUMS, scen), f32), pltpu....  5.09 us
  transfers between devices with their start and end apart: 38, of which 23 were waited for; matrix products, arithmetic and copies ran while one was open for 0% of the time, Pallas kernels for 7%

profile of v2, /device:TPU:8, one launch (start us, length us, event | category | flops | bytes accessed | tf_op | source)
XLA Modules:
  0.0 123.7 jit_solution(15014704548855131286)
XLA Ops:
  0.7 5.1 %scores.4 = (f32[1568,128]{1,0:T(8,128)S(1)}, bf16[8,2,192,1024]{3,2,1,0:T(8,128)(2,1)S(1)}, bf16[1024,128]{1,0:T(8,128)(2,1)S(1)}) custom-call(s32[4]{0:T(128)S(1)} %pad_add_fusion.place_ref, s32[8,24]{1,0:T(8,128)} %bitcast.15, bf16[8,2,192,1024]{3,2,1,0:T(8,128)(2,1)} %bitcast.14, bf16[1024,128]{1,0:T(8,128)(2,1)} %prior_ref.1), custom_call_target="tpu_custom_call" | custom-call | flops 402653184 | bytes 1006632 | tf_op jit(solution)/shard_map/scores/pallas_call | solution.py:120
  5.9 2.2 %scores.5 = f32[1568,128]{1,0:T(8,128)S(1)} custom-call(bf16[8,2,192,1024]{3,2,1,0:T(8,128)(2,1)S(1)} %get-tuple-element.14.kept_ref, bf16[1024,128]{1,0:T(8,128)(2,1)S(1)} %get-tuple-element.15.weights_ref.current_ref), custom_call_target="tpu_custom_call" | custom-call | flops 402653184 | bytes 1006632 | tf_op jit(solution)/shard_map/scores/pallas_call | solution.py:136
  8.4 3.1 %collective-permute-start.1 = (bf16[416,128]{1,0:T(8,128)(2,1)S(1)}, bf16[416,128]{1,0:T(8,128)(2,1)S(1)}, u32[]{:S(2)}, u32[]{:S(2)}) collective-permute-start(bf16[416,128]{1,0:T(8,128)(2,1)S(1)} %constant_dynamic-update-slice_fusion), channel_id=1, source_target_pairs={{0,32},{4,36},{8,40},{12,44},{16,48},{20,52},{24,56},{28,60},{32,0... | collective-permute-start | bytes 319496 | tf_op jit(solution)/shard_map/sum_x/ppermute | solution.py:389
  11.6 1.1 collective-permute-start.3
  13.6 4.1 %collective-permute-done.3 = bf16[416,128]{1,0:T(8,128)(2,1)S(1)} collective-permute-done((bf16[416,128]{1,0:T(8,128)(2,1)S(1)}, bf16[416,128]{1,0:T(8,128)(2,1)S(1)}, u32[]{:S(2)}, u32[]{:S(2)}) %collective-permute-start.3) | collective-permute-done | bytes 106528 | tf_op jit(solution)/shard_map/sum_x/ppermute | solution.py:389
  19.0 2.0 %collective-permute-start.4 = (bf16[416,128]{1,0:T(8,128)(2,1)S(1)}, bf16[416,128]{1,0:T(8,128)(2,1)S(1)}, u32[]{:S(2)}, u32[]{:S(2)}) collective-permute-start(bf16[416,128]{1,0:T(8,128)(2,1)S(1)} %constant_dynamic-update-slice_fusion.12), channel_id=1, source_target_pairs={{0,8},{4,12},{8,0},{12,4},{16,24},{20,28},{24,16},{28,20},{32,40},... | collective-permute-start | bytes 319496 | tf_op jit(solution)/shard_map/sum_z/ppermute | solution.py:395
  21.0 2.7 %flip.1 = (bf16[1024,1536]{1,0:T(8,128)(2,1)S(1)}, bf16[1024,1536]{1,0:T(8,128)(2,1)S(1)}, f32[384,128]{1,0:T(8,128)S(1)}) custom-call(s32[4]{0:T(128)S(1)} %pad_add_fusion.place_ref, bf16[8,2,192,1024]{3,2,1,0:T(8,128)(2,1)S(1)} %get-tuple-element.14.kept_ref, s32[3072,128]{1,0:T(8,128)} %cost_ref.1, f32[392,128]{1,0:T(8,128)S(1)} %fusion.4.after_ref), custom_call_target="tpu_custom_call" | custom-call | flops 3221225472 | bytes 8053063 | tf_op jit(solution)/shard_map/flip/pallas_call | solution.py:188
  23.9 2.2 %collective-permute-start.7 = (bf16[416,128]{1,0:T(8,128)(2,1)S(1)}, bf16[416,128]{1,0:T(8,128)(2,1)S(1)}, u32[]{:S(2)}, u32[]{:S(2)}) collective-permute-start(bf16[416,128]{1,0:T(8,128)(2,1)S(1)} %constant_dynamic-update-slice_fusion.16), channel_id=1, source_target_pairs={{0,48},{4,52},{8,56},{12,60},{16,0},{20,4},{24,8},{28,12},{32,16},... | collective-permute-start | bytes 319496 | tf_op jit(solution)/shard_map/gather/ppermute | solution.py:402
  27.8 6.2 %collective-permute-done.5 = bf16[416,128]{1,0:T(8,128)(2,1)S(1)} collective-permute-done((bf16[416,128]{1,0:T(8,128)(2,1)S(1)}, bf16[416,128]{1,0:T(8,128)(2,1)S(1)}, u32[]{:S(2)}, u32[]{:S(2)}) %collective-permute-start.5) | collective-permute-done | bytes 106528 | tf_op jit(solution)/shard_map/gather/ppermute | solution.py:402
  35.0 1.6 %collective-permute-start.10 = (f32[8,128]{1,0:T(8,128)S(1)}, f32[8,128]{1,0:T(8,128)S(1)}, u32[]{:S(2)}, u32[]{:S(2)}) collective-permute-start(f32[8,128]{1,0:T(8,128)S(1)} %total.2), channel_id=1, source_target_pairs={{0,64},{64,128},{128,192},{192,0},{1,65},{65,129},{129,193},{193,1... | collective-permute-start | bytes 12296 | tf_op jit(solution)/shard_map/total/ppermute | solution.py:364
  36.6 3.5 %collective-permute-start.9 = (f32[8,128]{1,0:T(8,128)S(1)}, f32[8,128]{1,0:T(8,128)S(1)}, u32[]{:S(2)}, u32[]{:S(2)}) collective-permute-start(f32[8,128]{1,0:T(8,128)S(1)} %total.2), channel_id=1, source_target_pairs={{0,128},{64,192},{128,0},{192,64},{1,129},{65,193},{129,1},{193,65... | collective-permute-start | bytes 12296 | tf_op jit(solution)/shard_map/total/ppermute | solution.py:364
  40.1 1.1 loads.4
  41.7 1.1 loads.5
  43.2 1.5 %collective-permute-start.14 = (f16[1040,128]{1,0:T(8,128)(2,1)S(1)}, f16[1040,128]{1,0:T(8,128)(2,1)S(1)}, u32[]{:S(2)}, u32[]{:S(2)}) collective-permute-start(f16[1040,128]{1,0:T(8,128)(2,1)S(1)} %get-tuple-element.63), channel_id=1, source_target_pairs={{0,192},{64,0},{128,64},{192,128},{1,193},{65,1},{129,65},{193,129... | collective-permute-start | bytes 798728 | tf_op jit(solution)/shard_map/sum_y/ppermute | solution.py:418
  44.7 2.2 %collective-permute-start.13 = (f16[1040,128]{1,0:T(8,128)(2,1)S(1)}, f16[1040,128]{1,0:T(8,128)(2,1)S(1)}, u32[]{:S(2)}, u32[]{:S(2)}) collective-permute-start(f16[1040,128]{1,0:T(8,128)(2,1)S(1)} %get-tuple-element.63), channel_id=1, source_target_pairs={{0,128},{64,192},{128,0},{192,64},{1,129},{65,193},{129,1},{193,65... | collective-permute-start | bytes 798728 | tf_op jit(solution)/shard_map/sum_y/ppermute | solution.py:418
  46.9 2.5 %collective-permute-start.12 = (f16[1040,128]{1,0:T(8,128)(2,1)S(1)}, f16[1040,128]{1,0:T(8,128)(2,1)S(1)}, u32[]{:S(2)}, u32[]{:S(2)}) collective-permute-start(f16[1040,128]{1,0:T(8,128)(2,1)S(1)} %get-tuple-element.63), channel_id=1, source_target_pairs={{0,64},{64,128},{128,192},{192,0},{1,65},{65,129},{129,193},{193,1... | collective-permute-start | bytes 798728 | tf_op jit(solution)/shard_map/sum_y/ppermute | solution.py:418
  49.4 1.2 collective-permute-done.15
  50.6 5.9 %collective-permute-start.18 = (f32[8,128]{1,0:T(8,128)S(1)}, f32[8,128]{1,0:T(8,128)S(1)}, u32[]{:S(2)}, u32[]{:S(2)}) collective-permute-start(f32[8,128]{1,0:T(8,128)S(1)} %add.143), channel_id=1, source_target_pairs={{0,3},{1,0},{2,1},{3,2},{4,7},{5,4},{6,5},{7,6},{8,11},{9,8},{10,9... | collective-permute-start | bytes 12296 | tf_op jit(solution)/shard_map/total/ppermute | solution.py:364
  56.5 1.3 %collective-permute-done.18 = f32[8,128]{1,0:T(8,128)S(1)} collective-permute-done((f32[8,128]{1,0:T(8,128)S(1)}, f32[8,128]{1,0:T(8,128)S(1)}, u32[]{:S(2)}, u32[]{:S(2)}) %collective-permute-start.18) | collective-permute-done | bytes 4128 | tf_op jit(solution)/shard_map/total/ppermute | solution.py:364
  57.8 4.1 %collective-permute-start.16 = (f32[8,128]{1,0:T(8,128)S(1)}, f32[8,128]{1,0:T(8,128)S(1)}, u32[]{:S(2)}, u32[]{:S(2)}) collective-permute-start(f32[8,128]{1,0:T(8,128)S(1)} %add.143), channel_id=1, source_target_pairs={{0,2},{1,3},{2,0},{3,1},{4,6},{5,7},{6,4},{7,5},{8,10},{9,11},{10,... | collective-permute-start | bytes 12296 | tf_op jit(solution)/shard_map/total/ppermute | solution.py:364
  62.2 3.1 %collective-permute-done.16 = f32[8,128]{1,0:T(8,128)S(1)} collective-permute-done((f32[8,128]{1,0:T(8,128)S(1)}, f32[8,128]{1,0:T(8,128)S(1)}, u32[]{:S(2)}, u32[]{:S(2)}) %collective-permute-start.16) | collective-permute-done | bytes 4128 | tf_op jit(solution)/shard_map/total/ppermute | solution.py:364
  66.3 1.0 scores.7
  67.4 1.0 scores.6
  68.4 1.3 %collective-permute-done.19 = f32[1536,128]{1,0:T(8,128)S(1)} collective-permute-done((f32[1536,128]{1,0:T(8,128)S(1)}, f32[1536,128]{1,0:T(8,128)S(1)}, u32[]{:S(2)}, u32[]{:S(2)}) %collective-permute-start.19) | collective-permute-done | bytes 786464 | tf_op jit(solution)/shard_map/scores/ppermute | solution.py:386
  70.1 3.3 %collective-permute-start.22 = (s16[400,128]{1,0:T(8,128)(2,1)S(1)}, s16[400,128]{1,0:T(8,128)(2,1)S(1)}, u32[]{:S(2)}, u32[]{:S(2)}) collective-permute-start(s16[400,128]{1,0:T(8,128)(2,1)S(1)} %fusion.2), channel_id=1, source_target_pairs={{0,48},{4,52},{8,56},{12,60},{16,0},{20,4},{24,8},{28,12},{32,16},... | collective-permute-start | bytes 307208 | tf_op jit(solution)/shard_map/sum_x/ppermute | solution.py:389
  73.5 2.7 %collective-permute-done.21 = s16[400,128]{1,0:T(8,128)(2,1)S(1)} collective-permute-done((s16[400,128]{1,0:T(8,128)(2,1)S(1)}, s16[400,128]{1,0:T(8,128)(2,1)S(1)}, u32[]{:S(2)}, u32[]{:S(2)}) %collective-permute-start.21) | collective-permute-done | bytes 102432 | tf_op jit(solution)/shard_map/sum_x/ppermute | solution.py:389
  76.3 1.5 %collective-permute-done.22 = s16[400,128]{1,0:T(8,128)(2,1)S(1)} collective-permute-done((s16[400,128]{1,0:T(8,128)(2,1)S(1)}, s16[400,128]{1,0:T(8,128)(2,1)S(1)}, u32[]{:S(2)}, u32[]{:S(2)}) %collective-permute-start.22) | collective-permute-done | bytes 102432 | tf_op jit(solution)/shard_map/sum_x/ppermute | solution.py:389
  77.8 1.9 %collective-permute-done.20 = s16[400,128]{1,0:T(8,128)(2,1)S(1)} collective-permute-done((s16[400,128]{1,0:T(8,128)(2,1)S(1)}, s16[400,128]{1,0:T(8,128)(2,1)S(1)}, u32[]{:S(2)}, u32[]{:S(2)}) %collective-permute-start.20) | collective-permute-done | bytes 102432 | tf_op jit(solution)/shard_map/sum_x/ppermute | solution.py:389
  79.9 1.3 %collective-permute-start.23 = (s16[400,128]{1,0:T(8,128)(2,1)S(1)}, s16[400,128]{1,0:T(8,128)(2,1)S(1)}, u32[]{:S(2)}, u32[]{:S(2)}) collective-permute-start(s16[400,128]{1,0:T(8,128)(2,1)S(1)} %fusion.3), channel_id=1, source_target_pairs={{0,8},{4,12},{8,0},{12,4},{16,24},{20,28},{24,16},{28,20},{32,40},... | collective-permute-start | bytes 307208 | tf_op jit(solution)/shard_map/sum_z/ppermute | solution.py:395
  81.3 3.6 %collective-permute-done.23 = s16[400,128]{1,0:T(8,128)(2,1)S(1)} collective-permute-done((s16[400,128]{1,0:T(8,128)(2,1)S(1)}, s16[400,128]{1,0:T(8,128)(2,1)S(1)}, u32[]{:S(2)}, u32[]{:S(2)}) %collective-permute-start.23) | collective-permute-done | bytes 102432 | tf_op jit(solution)/shard_map/sum_z/ppermute | solution.py:395
  85.0 1.9 %collective-permute-start.26 = (bf16[384,128]{1,0:T(8,128)(2,1)S(1)}, bf16[384,128]{1,0:T(8,128)(2,1)S(1)}, u32[]{:S(2)}, u32[]{:S(2)}) collective-permute-start(bf16[384,128]{1,0:T(8,128)(2,1)S(1)} %get-tuple-element.31), channel_id=1, source_target_pairs={{0,48},{4,52},{8,56},{12,60},{16,0},{20,4},{24,8},{28,12},{32,16},... | collective-permute-start | bytes 294920 | tf_op jit(solution)/shard_map/gather/ppermute | solution.py:402
  86.9 1.0 collective-permute-start.24
  87.9 2.3 %collective-permute-done.26 = bf16[384,128]{1,0:T(8,128)(2,1)S(1)} collective-permute-done((bf16[384,128]{1,0:T(8,128)(2,1)S(1)}, bf16[384,128]{1,0:T(8,128)(2,1)S(1)}, u32[]{:S(2)}, u32[]{:S(2)}) %collective-permute-start.26) | collective-permute-done | bytes 98336 | tf_op jit(solution)/shard_map/gather/ppermute | solution.py:402
  90.2 3.0 %collective-permute-done.25 = bf16[384,128]{1,0:T(8,128)(2,1)S(1)} collective-permute-done((bf16[384,128]{1,0:T(8,128)(2,1)S(1)}, bf16[384,128]{1,0:T(8,128)(2,1)S(1)}, u32[]{:S(2)}, u32[]{:S(2)}) %collective-permute-start.25) | collective-permute-done | bytes 98336 | tf_op jit(solution)/shard_map/gather/ppermute | solution.py:402
  94.4 2.0 %collective-permute-start.29 = (f32[8,128]{1,0:T(8,128)S(1)}, f32[8,128]{1,0:T(8,128)S(1)}, u32[]{:S(2)}, u32[]{:S(2)}) collective-permute-start(f32[8,128]{1,0:T(8,128)S(1)} %total.3), channel_id=1, source_target_pairs={{0,64},{64,128},{128,192},{192,0},{1,65},{65,129},{129,193},{193,1... | collective-permute-start | bytes 12296 | tf_op jit(solution)/shard_map/total/ppermute | solution.py:364
  96.4 1.8 %collective-permute-start.28 = (f32[8,128]{1,0:T(8,128)S(1)}, f32[8,128]{1,0:T(8,128)S(1)}, u32[]{:S(2)}, u32[]{:S(2)}) collective-permute-start(f32[8,128]{1,0:T(8,128)S(1)} %total.3), channel_id=1, source_target_pairs={{0,128},{64,192},{128,0},{192,64},{1,129},{65,193},{129,1},{193,65... | collective-permute-start | bytes 12296 | tf_op jit(solution)/shard_map/total/ppermute | solution.py:364
  98.2 1.0 loads.6
  99.3 2.2 %collective-permute-done.28 = f32[8,128]{1,0:T(8,128)S(1)} collective-permute-done((f32[8,128]{1,0:T(8,128)S(1)}, f32[8,128]{1,0:T(8,128)S(1)}, u32[]{:S(2)}, u32[]{:S(2)}) %collective-permute-start.28) | collective-permute-done | bytes 4128 | tf_op jit(solution)/shard_map/total/ppermute | solution.py:364
  101.5 1.1 loads.7
  103.2 1.8 %collective-permute-start.32 = (f16[1040,128]{1,0:T(8,128)(2,1)S(1)}, f16[1040,128]{1,0:T(8,128)(2,1)S(1)}, u32[]{:S(2)}, u32[]{:S(2)}) collective-permute-start(f16[1040,128]{1,0:T(8,128)(2,1)S(1)} %get-tuple-element.61), channel_id=1, source_target_pairs={{0,128},{64,192},{128,0},{192,64},{1,129},{65,193},{129,1},{193,65... | collective-permute-start | bytes 798728 | tf_op jit(solution)/shard_map/sum_y/ppermute | solution.py:418
  105.0 2.5 %collective-permute-start.31 = (f16[1040,128]{1,0:T(8,128)(2,1)S(1)}, f16[1040,128]{1,0:T(8,128)(2,1)S(1)}, u32[]{:S(2)}, u32[]{:S(2)}) collective-permute-start(f16[1040,128]{1,0:T(8,128)(2,1)S(1)} %get-tuple-element.61), channel_id=1, source_target_pairs={{0,64},{64,128},{128,192},{192,0},{1,65},{65,129},{129,193},{193,1... | collective-permute-start | bytes 798728 | tf_op jit(solution)/shard_map/sum_y/ppermute | solution.py:418
  107.5 1.2 collective-permute-done.34
  108.7 4.4 %collective-permute-start.37 = (f32[8,128]{1,0:T(8,128)S(1)}, f32[8,128]{1,0:T(8,128)S(1)}, u32[]{:S(2)}, u32[]{:S(2)}) collective-permute-start(f32[8,128]{1,0:T(8,128)S(1)} %add.159), channel_id=1, source_target_pairs={{0,3},{1,0},{2,1},{3,2},{4,7},{5,4},{6,5},{7,6},{8,11},{9,8},{10,9... | collective-permute-start | bytes 12296 | tf_op jit(solution)/shard_map/total/ppermute | solution.py:364
  113.1 1.3 %collective-permute-done.37 = f32[8,128]{1,0:T(8,128)S(1)} collective-permute-done((f32[8,128]{1,0:T(8,128)S(1)}, f32[8,128]{1,0:T(8,128)S(1)}, u32[]{:S(2)}, u32[]{:S(2)}) %collective-permute-start.37) | collective-permute-done | bytes 4128 | tf_op jit(solution)/shard_map/total/ppermute | solution.py:364
  114.4 2.9 %collective-permute-start.35 = (f32[8,128]{1,0:T(8,128)S(1)}, f32[8,128]{1,0:T(8,128)S(1)}, u32[]{:S(2)}, u32[]{:S(2)}) collective-permute-start(f32[8,128]{1,0:T(8,128)S(1)} %add.159), channel_id=1, source_target_pairs={{0,2},{1,3},{2,0},{3,1},{4,6},{5,7},{6,4},{7,5},{8,10},{9,11},{10,... | collective-permute-start | bytes 12296 | tf_op jit(solution)/shard_map/total/ppermute | solution.py:364
  117.3 1.5 %collective-permute-done.36 = f32[8,128]{1,0:T(8,128)S(1)} collective-permute-done((f32[8,128]{1,0:T(8,128)S(1)}, f32[8,128]{1,0:T(8,128)S(1)}, u32[]{:S(2)}, u32[]{:S(2)}) %collective-permute-start.36) | collective-permute-done | bytes 4128 | tf_op jit(solution)/shard_map/total/ppermute | solution.py:364
  118.8 3.1 %collective-permute-done.35 = f32[8,128]{1,0:T(8,128)S(1)} collective-permute-done((f32[8,128]{1,0:T(8,128)S(1)}, f32[8,128]{1,0:T(8,128)S(1)}, u32[]{:S(2)}, u32[]{:S(2)}) %collective-permute-start.35) | collective-permute-done | bytes 4128 | tf_op jit(solution)/shard_map/total/ppermute | solution.py:364
  122.1 1.6 %update.3 = (f32[1024,128]{1,0:T(8,128)}, f32[192,128]{1,0:T(8,128)}) custom-call(s32[4]{0:T(128)S(1)} %pad_add_fusion.place_ref, f32[1040,128]{1,0:T(8,128)S(1)} %get-tuple-element.62.zero, f32[1040,128]{1,0:T(8,128)S(1)} %convert_element_type.134.one, f32[1040,128]{1,0:T(8,128)S(1)} %convert_element_type.135.two, ...), custom_call_target="tpu_custom_call" | custom-call | flops 10000000 | bytes 25000 | tf_op jit(solution)/shard_map/update/pallas_call | solution.py:346
  (121 shorter events, 10.3 us)
Async XLA Ops:
  5.8 2.4 %collective-permute-start = (f32[1568,128]{1,0:T(8,128)S(1)}, f32[1568,128]{1,0:T(8,128)S(1)}, u32[]{:S(2)}, u32[]{:S(2)}) collective-permute-start(f32[1568,128]{1,0:T(8,128)S(1)} %get-tuple-element.16), channel_id=1, source_target_pairs={{0,4},{4,0},{8,12},{12,8},{16,20},{20,16},{24,28},{28,24},{32,36},... | collective-permute-start | bytes 2408456 | tf_op jit(solution)/shard_map/scores/ppermute | solution.py:386
  8.4 10.3 %collective-permute-start.1 = (bf16[416,128]{1,0:T(8,128)(2,1)S(1)}, bf16[416,128]{1,0:T(8,128)(2,1)S(1)}, u32[]{:S(2)}, u32[]{:S(2)}) collective-permute-start(bf16[416,128]{1,0:T(8,128)(2,1)S(1)} %constant_dynamic-update-slice_fusion), channel_id=1, source_target_pairs={{0,32},{4,36},{8,40},{12,44},{16,48},{20,52},{24,56},{28,60},{32,0... | collective-permute-start | bytes 319496 | tf_op jit(solution)/shard_map/sum_x/ppermute | solution.py:389
  11.6 6.2 %collective-permute-start.3 = (bf16[416,128]{1,0:T(8,128)(2,1)S(1)}, bf16[416,128]{1,0:T(8,128)(2,1)S(1)}, u32[]{:S(2)}, u32[]{:S(2)}) collective-permute-start(bf16[416,128]{1,0:T(8,128)(2,1)S(1)} %constant_dynamic-update-slice_fusion.8), channel_id=1, source_target_pairs={{0,48},{4,52},{8,56},{12,60},{16,0},{20,4},{24,8},{28,12},{32,16},... | collective-permute-start | bytes 319496 | tf_op jit(solution)/shard_map/sum_x/ppermute | solution.py:389
  12.7 6.0 %collective-permute-start.2 = (bf16[416,128]{1,0:T(8,128)(2,1)S(1)}, bf16[416,128]{1,0:T(8,128)(2,1)S(1)}, u32[]{:S(2)}, u32[]{:S(2)}) collective-permute-start(bf16[416,128]{1,0:T(8,128)(2,1)S(1)} %constant_dynamic-update-slice_fusion.4), channel_id=1, source_target_pairs={{0,16},{4,20},{8,24},{12,28},{16,32},{20,36},{24,40},{28,44},{32,4... | collective-permute-start | bytes 319496 | tf_op jit(solution)/shard_map/sum_x/ppermute | solution.py:389
  19.0 4.8 %collective-permute-start.4 = (bf16[416,128]{1,0:T(8,128)(2,1)S(1)}, bf16[416,128]{1,0:T(8,128)(2,1)S(1)}, u32[]{:S(2)}, u32[]{:S(2)}) collective-permute-start(bf16[416,128]{1,0:T(8,128)(2,1)S(1)} %constant_dynamic-update-slice_fusion.12), channel_id=1, source_target_pairs={{0,8},{4,12},{8,0},{12,4},{16,24},{20,28},{24,16},{28,20},{32,40},... | collective-permute-start | bytes 319496 | tf_op jit(solution)/shard_map/sum_z/ppermute | solution.py:395
  23.9 10.1 %collective-permute-start.7 = (bf16[416,128]{1,0:T(8,128)(2,1)S(1)}, bf16[416,128]{1,0:T(8,128)(2,1)S(1)}, u32[]{:S(2)}, u32[]{:S(2)}) collective-permute-start(bf16[416,128]{1,0:T(8,128)(2,1)S(1)} %constant_dynamic-update-slice_fusion.16), channel_id=1, source_target_pairs={{0,48},{4,52},{8,56},{12,60},{16,0},{20,4},{24,8},{28,12},{32,16},... | collective-permute-start | bytes 319496 | tf_op jit(solution)/shard_map/gather/ppermute | solution.py:402
  26.2 7.8 %collective-permute-start.6 = (bf16[416,128]{1,0:T(8,128)(2,1)S(1)}, bf16[416,128]{1,0:T(8,128)(2,1)S(1)}, u32[]{:S(2)}, u32[]{:S(2)}) collective-permute-start(bf16[416,128]{1,0:T(8,128)(2,1)S(1)} %constant_dynamic-update-slice_fusion.16), channel_id=1, source_target_pairs={{0,32},{4,36},{8,40},{12,44},{16,48},{20,52},{24,56},{28,60},{32,0... | collective-permute-start | bytes 319496 | tf_op jit(solution)/shard_map/gather/ppermute | solution.py:402
  27.0 7.0 %collective-permute-start.5 = (bf16[416,128]{1,0:T(8,128)(2,1)S(1)}, bf16[416,128]{1,0:T(8,128)(2,1)S(1)}, u32[]{:S(2)}, u32[]{:S(2)}) collective-permute-start(bf16[416,128]{1,0:T(8,128)(2,1)S(1)} %constant_dynamic-update-slice_fusion.16), channel_id=1, source_target_pairs={{0,16},{4,20},{8,24},{12,28},{16,32},{20,36},{24,40},{28,44},{32,4... | collective-permute-start | bytes 319496 | tf_op jit(solution)/shard_map/gather/ppermute | solution.py:402
  34.0 7.7 %collective-permute-start.8 = (bf16[1664,128]{1,0:T(8,128)(2,1)S(1)}, bf16[1664,128]{1,0:T(8,128)(2,1)S(1)}, u32[]{:S(2)}, u32[]{:S(2)}) collective-permute-start(bf16[1664,128]{1,0:T(8,128)(2,1)S(1)} %constant_dynamic-update-slice_fusion.21.low_ref.sums_ref), channel_id=1, source_target_pairs={{0,4},{4,0},{8,12},{12,8},{16,20},{20,16},{24,28},{28,24},{32,36},... | collective-permute-start | bytes 1277960 | tf_op jit(solution)/shard_map/gather/ppermute | solution.py:404
  34.5 6.7 %collective-permute-start.11 = (f32[8,128]{1,0:T(8,128)S(1)}, f32[8,128]{1,0:T(8,128)S(1)}, u32[]{:S(2)}, u32[]{:S(2)}) collective-permute-start(f32[8,128]{1,0:T(8,128)S(1)} %total.2), channel_id=1, source_target_pairs={{0,192},{64,0},{128,64},{192,128},{1,193},{65,1},{129,65},{193,129... | collective-permute-start | bytes 12296 | tf_op jit(solution)/shard_map/total/ppermute | solution.py:364
  35.0 6.2 %collective-permute-start.10 = (f32[8,128]{1,0:T(8,128)S(1)}, f32[8,128]{1,0:T(8,128)S(1)}, u32[]{:S(2)}, u32[]{:S(2)}) collective-permute-start(f32[8,128]{1,0:T(8,128)S(1)} %total.2), channel_id=1, source_target_pairs={{0,64},{64,128},{128,192},{192,0},{1,65},{65,129},{129,193},{193,1... | collective-permute-start | bytes 12296 | tf_op jit(solution)/shard_map/total/ppermute | solution.py:364
  36.6 5.1 %collective-permute-start.9 = (f32[8,128]{1,0:T(8,128)S(1)}, f32[8,128]{1,0:T(8,128)S(1)}, u32[]{:S(2)}, u32[]{:S(2)}) collective-permute-start(f32[8,128]{1,0:T(8,128)S(1)} %total.2), channel_id=1, source_target_pairs={{0,128},{64,192},{128,0},{192,64},{1,129},{65,193},{129,1},{193,65... | collective-permute-start | bytes 12296 | tf_op jit(solution)/shard_map/total/ppermute | solution.py:364
  43.2 22.2 %collective-permute-start.14 = (f16[1040,128]{1,0:T(8,128)(2,1)S(1)}, f16[1040,128]{1,0:T(8,128)(2,1)S(1)}, u32[]{:S(2)}, u32[]{:S(2)}) collective-permute-start(f16[1040,128]{1,0:T(8,128)(2,1)S(1)} %get-tuple-element.63), channel_id=1, source_target_pairs={{0,192},{64,0},{128,64},{192,128},{1,193},{65,1},{129,65},{193,129... | collective-permute-start | bytes 798728 | tf_op jit(solution)/shard_map/sum_y/ppermute | solution.py:418
  44.7 20.7 %collective-permute-start.13 = (f16[1040,128]{1,0:T(8,128)(2,1)S(1)}, f16[1040,128]{1,0:T(8,128)(2,1)S(1)}, u32[]{:S(2)}, u32[]{:S(2)}) collective-permute-start(f16[1040,128]{1,0:T(8,128)(2,1)S(1)} %get-tuple-element.63), channel_id=1, source_target_pairs={{0,128},{64,192},{128,0},{192,64},{1,129},{65,193},{129,1},{193,65... | collective-permute-start | bytes 798728 | tf_op jit(solution)/shard_map/sum_y/ppermute | solution.py:418
  46.9 18.6 %collective-permute-start.12 = (f16[1040,128]{1,0:T(8,128)(2,1)S(1)}, f16[1040,128]{1,0:T(8,128)(2,1)S(1)}, u32[]{:S(2)}, u32[]{:S(2)}) collective-permute-start(f16[1040,128]{1,0:T(8,128)(2,1)S(1)} %get-tuple-element.63), channel_id=1, source_target_pairs={{0,64},{64,128},{128,192},{192,0},{1,65},{65,129},{129,193},{193,1... | collective-permute-start | bytes 798728 | tf_op jit(solution)/shard_map/sum_y/ppermute | solution.py:418
  49.4 1.2 collective-permute-start.15
  50.6 7.2 %collective-permute-start.18 = (f32[8,128]{1,0:T(8,128)S(1)}, f32[8,128]{1,0:T(8,128)S(1)}, u32[]{:S(2)}, u32[]{:S(2)}) collective-permute-start(f32[8,128]{1,0:T(8,128)S(1)} %add.143), channel_id=1, source_target_pairs={{0,3},{1,0},{2,1},{3,2},{4,7},{5,4},{6,5},{7,6},{8,11},{9,8},{10,9... | collective-permute-start | bytes 12296 | tf_op jit(solution)/shard_map/total/ppermute | solution.py:364
  56.5 5.7 %collective-permute-start.17 = (f32[8,128]{1,0:T(8,128)S(1)}, f32[8,128]{1,0:T(8,128)S(1)}, u32[]{:S(2)}, u32[]{:S(2)}) collective-permute-start(f32[8,128]{1,0:T(8,128)S(1)} %add.143), channel_id=1, source_target_pairs={{0,1},{1,2},{2,3},{3,0},{4,5},{5,6},{6,7},{7,4},{8,9},{9,10},{10,1... | collective-permute-start | bytes 12296 | tf_op jit(solution)/shard_map/total/ppermute | solution.py:364
  57.8 7.5 %collective-permute-start.16 = (f32[8,128]{1,0:T(8,128)S(1)}, f32[8,128]{1,0:T(8,128)S(1)}, u32[]{:S(2)}, u32[]{:S(2)}) collective-permute-start(f32[8,128]{1,0:T(8,128)S(1)} %add.143), channel_id=1, source_target_pairs={{0,2},{1,3},{2,0},{3,1},{4,6},{5,7},{6,4},{7,5},{8,10},{9,11},{10,... | collective-permute-start | bytes 12296 | tf_op jit(solution)/shard_map/total/ppermute | solution.py:364
  67.3 2.4 %collective-permute-start.19 = (f32[1536,128]{1,0:T(8,128)S(1)}, f32[1536,128]{1,0:T(8,128)S(1)}, u32[]{:S(2)}, u32[]{:S(2)}) collective-permute-start(f32[1536,128]{1,0:T(8,128)S(1)} %scores.7), channel_id=1, source_target_pairs={{0,4},{4,0},{8,12},{12,8},{16,20},{20,16},{24,28},{28,24},{32,36},... | collective-permute-start | bytes 2359304 | tf_op jit(solution)/shard_map/scores/ppermute | solution.py:386
  70.0 6.2 %collective-permute-start.21 = (s16[400,128]{1,0:T(8,128)(2,1)S(1)}, s16[400,128]{1,0:T(8,128)(2,1)S(1)}, u32[]{:S(2)}, u32[]{:S(2)}) collective-permute-start(s16[400,128]{1,0:T(8,128)(2,1)S(1)} %fusion.1), channel_id=1, source_target_pairs={{0,16},{4,20},{8,24},{12,28},{16,32},{20,36},{24,40},{28,44},{32,4... | collective-permute-start | bytes 307208 | tf_op jit(solution)/shard_map/sum_x/ppermute | solution.py:389
  70.1 7.6 %collective-permute-start.22 = (s16[400,128]{1,0:T(8,128)(2,1)S(1)}, s16[400,128]{1,0:T(8,128)(2,1)S(1)}, u32[]{:S(2)}, u32[]{:S(2)}) collective-permute-start(s16[400,128]{1,0:T(8,128)(2,1)S(1)} %fusion.2), channel_id=1, source_target_pairs={{0,48},{4,52},{8,56},{12,60},{16,0},{20,4},{24,8},{28,12},{32,16},... | collective-permute-start | bytes 307208 | tf_op jit(solution)/shard_map/sum_x/ppermute | solution.py:389
  73.4 6.3 %collective-permute-start.20 = (s16[400,128]{1,0:T(8,128)(2,1)S(1)}, s16[400,128]{1,0:T(8,128)(2,1)S(1)}, u32[]{:S(2)}, u32[]{:S(2)}) collective-permute-start(s16[400,128]{1,0:T(8,128)(2,1)S(1)} %fusion), channel_id=1, source_target_pairs={{0,32},{4,36},{8,40},{12,44},{16,48},{20,52},{24,56},{28,60},{32,0... | collective-permute-start | bytes 307208 | tf_op jit(solution)/shard_map/sum_x/ppermute | solution.py:389
  79.9 5.0 %collective-permute-start.23 = (s16[400,128]{1,0:T(8,128)(2,1)S(1)}, s16[400,128]{1,0:T(8,128)(2,1)S(1)}, u32[]{:S(2)}, u32[]{:S(2)}) collective-permute-start(s16[400,128]{1,0:T(8,128)(2,1)S(1)} %fusion.3), channel_id=1, source_target_pairs={{0,8},{4,12},{8,0},{12,4},{16,24},{20,28},{24,16},{28,20},{32,40},... | collective-permute-start | bytes 307208 | tf_op jit(solution)/shard_map/sum_z/ppermute | solution.py:395
  85.0 5.1 %collective-permute-start.26 = (bf16[384,128]{1,0:T(8,128)(2,1)S(1)}, bf16[384,128]{1,0:T(8,128)(2,1)S(1)}, u32[]{:S(2)}, u32[]{:S(2)}) collective-permute-start(bf16[384,128]{1,0:T(8,128)(2,1)S(1)} %get-tuple-element.31), channel_id=1, source_target_pairs={{0,48},{4,52},{8,56},{12,60},{16,0},{20,4},{24,8},{28,12},{32,16},... | collective-permute-start | bytes 294920 | tf_op jit(solution)/shard_map/gather/ppermute | solution.py:402
  86.9 6.2 %collective-permute-start.25 = (bf16[384,128]{1,0:T(8,128)(2,1)S(1)}, bf16[384,128]{1,0:T(8,128)(2,1)S(1)}, u32[]{:S(2)}, u32[]{:S(2)}) collective-permute-start(bf16[384,128]{1,0:T(8,128)(2,1)S(1)} %get-tuple-element.31), channel_id=1, source_target_pairs={{0,32},{4,36},{8,40},{12,44},{16,48},{20,52},{24,56},{28,60},{32,0... | collective-permute-start | bytes 294920 | tf_op jit(solution)/shard_map/gather/ppermute | solution.py:402
  86.9 6.9 %collective-permute-start.24 = (bf16[384,128]{1,0:T(8,128)(2,1)S(1)}, bf16[384,128]{1,0:T(8,128)(2,1)S(1)}, u32[]{:S(2)}, u32[]{:S(2)}) collective-permute-start(bf16[384,128]{1,0:T(8,128)(2,1)S(1)} %get-tuple-element.31), channel_id=1, source_target_pairs={{0,16},{4,20},{8,24},{12,28},{16,32},{20,36},{24,40},{28,44},{32,4... | collective-permute-start | bytes 294920 | tf_op jit(solution)/shard_map/gather/ppermute | solution.py:402
  93.8 7.7 %collective-permute-start.27 = (bf16[1536,128]{1,0:T(8,128)(2,1)S(1)}, bf16[1536,128]{1,0:T(8,128)(2,1)S(1)}, u32[]{:S(2)}, u32[]{:S(2)}) collective-permute-start(bf16[1536,128]{1,0:T(8,128)(2,1)S(1)} %pad_maximum_fusion.low_ref), channel_id=1, source_target_pairs={{0,4},{4,0},{8,12},{12,8},{16,20},{20,16},{24,28},{28,24},{32,36},... | collective-permute-start | bytes 1179656 | tf_op jit(solution)/shard_map/gather/ppermute | solution.py:404
  94.3 5.0 %collective-permute-start.30 = (f32[8,128]{1,0:T(8,128)S(1)}, f32[8,128]{1,0:T(8,128)S(1)}, u32[]{:S(2)}, u32[]{:S(2)}) collective-permute-start(f32[8,128]{1,0:T(8,128)S(1)} %total.3), channel_id=1, source_target_pairs={{0,192},{64,0},{128,64},{192,128},{1,193},{65,1},{129,65},{193,129... | collective-permute-start | bytes 12296 | tf_op jit(solution)/shard_map/total/ppermute | solution.py:364
  94.4 4.9 %collective-permute-start.29 = (f32[8,128]{1,0:T(8,128)S(1)}, f32[8,128]{1,0:T(8,128)S(1)}, u32[]{:S(2)}, u32[]{:S(2)}) collective-permute-start(f32[8,128]{1,0:T(8,128)S(1)} %total.3), channel_id=1, source_target_pairs={{0,64},{64,128},{128,192},{192,0},{1,65},{65,129},{129,193},{193,1... | collective-permute-start | bytes 12296 | tf_op jit(solution)/shard_map/total/ppermute | solution.py:364
  96.4 5.1 %collective-permute-start.28 = (f32[8,128]{1,0:T(8,128)S(1)}, f32[8,128]{1,0:T(8,128)S(1)}, u32[]{:S(2)}, u32[]{:S(2)}) collective-permute-start(f32[8,128]{1,0:T(8,128)S(1)} %total.3), channel_id=1, source_target_pairs={{0,128},{64,192},{128,0},{192,64},{1,129},{65,193},{129,1},{193,65... | collective-permute-start | bytes 12296 | tf_op jit(solution)/shard_map/total/ppermute | solution.py:364
  103.0 18.9 %collective-permute-start.33 = (f16[1040,128]{1,0:T(8,128)(2,1)S(1)}, f16[1040,128]{1,0:T(8,128)(2,1)S(1)}, u32[]{:S(2)}, u32[]{:S(2)}) collective-permute-start(f16[1040,128]{1,0:T(8,128)(2,1)S(1)} %get-tuple-element.61), channel_id=1, source_target_pairs={{0,192},{64,0},{128,64},{192,128},{1,193},{65,1},{129,65},{193,129... | collective-permute-start | bytes 798728 | tf_op jit(solution)/shard_map/sum_y/ppermute | solution.py:418
  103.2 18.8 %collective-permute-start.32 = (f16[1040,128]{1,0:T(8,128)(2,1)S(1)}, f16[1040,128]{1,0:T(8,128)(2,1)S(1)}, u32[]{:S(2)}, u32[]{:S(2)}) collective-permute-start(f16[1040,128]{1,0:T(8,128)(2,1)S(1)} %get-tuple-element.61), channel_id=1, source_target_pairs={{0,128},{64,192},{128,0},{192,64},{1,129},{65,193},{129,1},{193,65... | collective-permute-start | bytes 798728 | tf_op jit(solution)/shard_map/sum_y/ppermute | solution.py:418
  105.0 17.1 %collective-permute-start.31 = (f16[1040,128]{1,0:T(8,128)(2,1)S(1)}, f16[1040,128]{1,0:T(8,128)(2,1)S(1)}, u32[]{:S(2)}, u32[]{:S(2)}) collective-permute-start(f16[1040,128]{1,0:T(8,128)(2,1)S(1)} %get-tuple-element.61), channel_id=1, source_target_pairs={{0,64},{64,128},{128,192},{192,0},{1,65},{65,129},{129,193},{193,1... | collective-permute-start | bytes 798728 | tf_op jit(solution)/shard_map/sum_y/ppermute | solution.py:418
  107.5 1.2 collective-permute-start.34
  108.7 5.7 %collective-permute-start.37 = (f32[8,128]{1,0:T(8,128)S(1)}, f32[8,128]{1,0:T(8,128)S(1)}, u32[]{:S(2)}, u32[]{:S(2)}) collective-permute-start(f32[8,128]{1,0:T(8,128)S(1)} %add.159), channel_id=1, source_target_pairs={{0,3},{1,0},{2,1},{3,2},{4,7},{5,4},{6,5},{7,6},{8,11},{9,8},{10,9... | collective-permute-start | bytes 12296 | tf_op jit(solution)/shard_map/total/ppermute | solution.py:364
  113.1 5.7 %collective-permute-start.36 = (f32[8,128]{1,0:T(8,128)S(1)}, f32[8,128]{1,0:T(8,128)S(1)}, u32[]{:S(2)}, u32[]{:S(2)}) collective-permute-start(f32[8,128]{1,0:T(8,128)S(1)} %add.159), channel_id=1, source_target_pairs={{0,1},{1,2},{2,3},{3,0},{4,5},{5,6},{6,7},{7,4},{8,9},{9,10},{10,1... | collective-permute-start | bytes 12296 | tf_op jit(solution)/shard_map/total/ppermute | solution.py:364
  114.4 7.5 %collective-permute-start.35 = (f32[8,128]{1,0:T(8,128)S(1)}, f32[8,128]{1,0:T(8,128)S(1)}, u32[]{:S(2)}, u32[]{:S(2)}) collective-permute-start(f32[8,128]{1,0:T(8,128)S(1)} %add.159), channel_id=1, source_target_pairs={{0,2},{1,3},{2,0},{3,1},{4,6},{5,7},{6,4},{7,5},{8,10},{9,11},{10,... | collective-permute-start | bytes 12296 | tf_op jit(solution)/shard_map/total/ppermute | solution.py:364
